TPU v7x, 256 devices: a whole 4x4x8 slice. The times are simulated.
256 devices in a mesh: ctx: 32 (over z, x_hi, core), tp: 8 (over y, x_lo).
Axes of the slice: x: 4 (x_hi: 2, x_lo: 2; x = x_hi * 2 + x_lo), y: 4, z: 8, core: 2. Of those that a mesh axis runs over, the one named last changes fastest.
Arguments:
- query_in: bfloat16 [4096, 8192], P('ctx', 'tp'), may hold values from -6 to 6
- key_in: bfloat16 [4096, 8192], P('ctx', 'tp'), may hold values from -6 to 6
- value_in: bfloat16 [4096, 8192], P('ctx', 'tp'), may hold values from -6 to 6
- short_query: float32 [3, 8192], P(None, 'tp'), may hold values from -3 to 3
- short_key: float32 [3, 8192], P(None, 'tp'), may hold values from -3 to 3
- short_value: float32 [3, 8192], P(None, 'tp'), may hold values from -3 to 3
- long_filter: float32 [4096, 8192], P('ctx', 'tp'), may hold values from -0.09375 to 0.09375
- skip_gain: float32 [8192], P('tp'), may hold values from 0.5 to 1.5
- out_weight: bfloat16 [8192, 4096], P('tp', 'ctx'), may hold values from -0.125 to 0.125
- cotangent: bfloat16 [4096, 4096], P('ctx', 'tp'), may hold values from -4 to 4
Outputs:
- mixed_out: bfloat16 [4096, 4096], P('ctx', 'tp')
- grad_query: bfloat16 [4096, 8192], P('ctx', 'tp')
- grad_key: bfloat16 [4096, 8192], P('ctx', 'tp')
- grad_value: bfloat16 [4096, 8192], P('ctx', 'tp')
- grad_filter: bfloat16 [4096, 8192], P('ctx', 'tp')
- grad_skip: float32 [8192], P('tp')
- grad_short: float32 [3, 3, 8192], P(None, None, 'tp')
All inputs are finite; a program needn't handle non-finite values.
Results may differ from a plain program's by a relative error of at most 0.0049.
Values may be sent and summed in bfloat16 or wider, within the bound.
A program may use at most 128 MiB of HBM per device.

v0:
```python
import jax
import jax.numpy as jnp
from jax import lax
from jax.sharding import PartitionSpec as P


def shifted(shard, axis, by):
    size = lax.axis_size(axis)
    pairs = [(i, i + by) for i in range(size) if 0 <= i + by < size]
    return lax.ppermute(shard, axis, pairs)


def mixer(form, left, right):
    return jnp.einsum(form, left, right, precision=lax.Precision.HIGHEST)


def angles(first, second, period):
    turns = first[:, None] * second[None, :] % period
    theta = 2.0 * jnp.pi / period * turns.astype(jnp.float32)
    return (jnp.cos(theta), jnp.sin(theta))


def outer_forward(field, j_index, total):
    blocks = field.shape[1]
    m_index = jnp.arange(blocks, dtype=jnp.int32)
    q_index = jnp.arange(2 * blocks, dtype=jnp.int32)
    cos_a, sin_a = angles(q_index, m_index, 2 * blocks)
    y_real = mixer("qm,bmjc->bqjc", cos_a, field)
    y_imag = -mixer("qm,bmjc->bqjc", sin_a, field)
    cos_t, sin_t = angles(q_index, j_index, total)
    cos_t = cos_t[None, :, :, None]
    sin_t = sin_t[None, :, :, None]
    return jnp.stack([y_real * cos_t + y_imag * sin_t, y_imag * cos_t - y_real * sin_t])


def inner_forward(pair):
    seq_len = pair.shape[3]
    index = jnp.arange(seq_len, dtype=jnp.int32)
    cos_b, sin_b = angles(index, index, seq_len)
    real = mixer("pj,bqjc->bqpc", cos_b, pair[0]) + mixer("pj,bqjc->bqpc", sin_b, pair[1])
    imag = mixer("pj,bqjc->bqpc", cos_b, pair[1]) - mixer("pj,bqjc->bqpc", sin_b, pair[0])
    return (real, imag)


def inner_inverse(real, imag, q_index, total):
    seq_len = real.shape[2]
    index = jnp.arange(seq_len, dtype=jnp.int32)
    cos_b, sin_b = angles(index, index, seq_len)
    y_real = mixer("jp,bqpc->bqjc", cos_b, real) - mixer("jp,bqpc->bqjc", sin_b, imag)
    y_imag = mixer("jp,bqpc->bqjc", cos_b, imag) + mixer("jp,bqpc->bqjc", sin_b, real)
    cos_t, sin_t = angles(q_index, index, total)
    cos_t = cos_t[None, :, :, None]
    sin_t = sin_t[None, :, :, None]
    return jnp.stack([y_real * cos_t - y_imag * sin_t, y_real * sin_t + y_imag * cos_t])


def outer_inverse(pair, total):
    blocks = pair.shape[2] // 2
    m_index = jnp.arange(blocks, dtype=jnp.int32)
    q_index = jnp.arange(2 * blocks, dtype=jnp.int32)
    cos_a, sin_a = angles(m_index, q_index, 2 * blocks)
    return (mixer("mq,bqjc->bmjc", cos_a, pair[0]) - mixer("mq,bqjc->bmjc", sin_a, pair[1])) / total


def spectrum_channels(field):
    count = lax.axis_size("ctx")
    seq_len = field.shape[1]
    total = 2 * count * seq_len
    spread = lax.all_to_all(field, "ctx", split_axis=2, concat_axis=1, tiled=True)
    blocks = spread.reshape(field.shape[0], count, seq_len, spread.shape[2])
    pair = outer_forward(blocks, jnp.arange(seq_len, dtype=jnp.int32), total)
    return inner_forward(pair)


def signal_channels(real, imag):
    count = real.shape[1] // 2
    seq_len = real.shape[2]
    total = 2 * count * seq_len
    q_index = jnp.arange(real.shape[1], dtype=jnp.int32)
    pair = inner_inverse(real, imag, q_index, total)
    blocks = outer_inverse(pair, total)
    joined = blocks.reshape(real.shape[0], count * seq_len, real.shape[3])
    return lax.all_to_all(joined, "ctx", split_axis=1, concat_axis=2, tiled=True)


def forward_any(field):
    return spectrum_channels(field)


def inverse_any(real, imag):
    return signal_channels(real, imag)


def local(
    query_in,
    key_in,
    value_in,
    short_query,
    short_key,
    short_value,
    long_filter,
    skip_gain,
    out_weight,
    cotangent,
):
    seq_len = query_in.shape[0]
    inputs = jnp.stack([query_in, key_in, value_in])
    earlier = shifted(inputs[:, seq_len - 2 :], "ctx", 1)
    extended = jnp.concatenate([earlier, inputs], axis=1).astype(jnp.float32)
    taps = jnp.stack([short_query, short_key, short_value])
    shorts = (
        taps[:, 0, None] * extended[:, 2:]
        + taps[:, 1, None] * extended[:, 1 : seq_len + 1]
        + taps[:, 2, None] * extended[:, :seq_len]
    )
    q_short = shorts[0]
    k_short = shorts[1]
    v_short = shorts[2]
    gated = k_short * v_short
    spec_real, spec_imag = forward_any(jnp.stack([gated, long_filter]))
    u_real, h_real = (spec_real[0], spec_real[1])
    u_imag, h_imag = (spec_imag[0], spec_imag[1])
    prod_real = u_real * h_real - u_imag * h_imag
    prod_imag = u_real * h_imag + u_imag * h_real
    convolved = inverse_any(prod_real[None], prod_imag[None])[0]
    mixing = convolved + skip_gain * gated
    hidden = (q_short * mixing).astype(jnp.bfloat16)
    partial_out = jnp.dot(
        hidden,
        lax.all_gather(out_weight, "ctx", axis=1, tiled=True),
        preferred_element_type=jnp.float32,
    )
    mixed_out = lax.psum_scatter(partial_out, "tp", scatter_dimension=1, tiled=True).astype(
        jnp.bfloat16
    )
    full_cotangent = lax.all_gather(cotangent, "tp", axis=1, tiled=True)
    grad_hidden = lax.dot_general(
        full_cotangent,
        lax.all_gather(out_weight, "ctx", axis=1, tiled=True),
        (((1,), (1,)), ((), ())),
        preferred_element_type=jnp.float32,
    )
    grad_qs = grad_hidden * mixing
    grad_mix = grad_hidden * q_short
    grad_spec_real, grad_spec_imag = forward_any(grad_mix[None])
    d_real = grad_spec_real[0]
    d_imag = grad_spec_imag[0]
    back_real = jnp.stack([h_real * d_real + h_imag * d_imag, u_real * d_real + u_imag * d_imag])
    back_imag = jnp.stack([h_real * d_imag - h_imag * d_real, u_real * d_imag - u_imag * d_real])
    results = inverse_any(back_real, back_imag)
    grad_gated = results[0] + skip_gain * grad_mix
    grad_filter = results[1].astype(jnp.bfloat16)
    grad_ks = grad_gated * v_short
    grad_vs = grad_gated * k_short
    grads = jnp.stack([grad_qs, grad_ks, grad_vs])
    later = shifted(grads[:, :2], "ctx", -1)
    padded = jnp.concatenate([grads, later], axis=1)
    returned = (
        taps[:, 0, None] * grads
        + taps[:, 1, None] * padded[:, 1 : seq_len + 1]
        + taps[:, 2, None] * padded[:, 2:]
    )
    tap_terms = jnp.stack(
        [
            jnp.sum(grads * extended[:, 2 - offset : 2 - offset + seq_len], axis=1)
            for offset in range(3)
        ],
        axis=1,
    )
    skip_term = jnp.sum(grad_mix * gated, axis=0)
    grad_skip, grad_short = lax.psum((skip_term, tap_terms), "ctx")
    return (
        mixed_out,
        returned[0].astype(jnp.bfloat16),
        returned[1].astype(jnp.bfloat16),
        returned[2].astype(jnp.bfloat16),
        grad_filter,
        grad_skip,
        grad_short,
    )


def solution(mesh):
    in_specs = (
        P("ctx", "tp"),
        P("ctx", "tp"),
        P("ctx", "tp"),
        P(None, "tp"),
        P(None, "tp"),
        P(None, "tp"),
        P("ctx", "tp"),
        P("tp"),
        P("tp", "ctx"),
        P("ctx", "tp"),
    )
    out_specs = (
        P("ctx", "tp"),
        P("ctx", "tp"),
        P("ctx", "tp"),
        P("ctx", "tp"),
        P("ctx", "tp"),
        P("tp"),
        P(None, None, "tp"),
    )
    return jax.shard_map(local, mesh=mesh, in_specs=in_specs, out_specs=out_specs, check_vma=False)
```

profile of v0, /device:TPU:128, one launch (start us, length us, event | category | flops | bytes accessed | tf_op | source)
XLA Modules:
  0.0 538.1 jit_solution(14363479606606220582)
XLA Ops:
  9.4 1.9 collective-permute-start
  12.3 5.7 %collective-permute-done = bf16[3,2,1024]{2,1,0:T(2,128)(2,1)S(1)} collective-permute-done((bf16[3,2,1024]{2,1,0:T(2,128)(2,1)S(1)}, bf16[3,2,1024]{2,1,0:T(2,128)(2,1)S(1)}, u32[]{:S(2)}, u32[]{:S(2)}) %collective-permute-start) | collective-permute-done | bytes 12320 | tf_op jit(solution)/shard_map/ppermute | solution.py:10
  21.5 2.3 copy.105
  23.9 7.8 %all-to-all-start = ((f32[2,128,1024]{1,0,2:T(2,128)}), f32[2,128,1024]{1,0,2:T(2,128)}, u32[]{:S(2)}, u32[]{:S(2)}) async-start(f32[2,128,1024]{1,0,2:T(2,128)} %copy.105), calls=%async_computation | async-start | bytes 2097152 | tf_op jit(solution)/shard_map/all_to_all | solution.py:69
  31.8 25.7 %all-to-all-done = f32[2,128,1024]{1,0,2:T(2,128)} async-done(((f32[2,128,1024]{1,0,2:T(2,128)}), f32[2,128,1024]{1,0,2:T(2,128)}, u32[]{:S(2)}, u32[]{:S(2)}) %all-to-all-start) | async-done | bytes 1048608 | tf_op jit(solution)/shard_map/all_to_all | solution.py:69
  57.5 3.7 fusion.49
  61.2 5.5 %fusion = (f32[2,64,128,32]{2,1,3,0:T(8,128)}, f32[2,64,128,32]{2,1,3,0:T(8,128)S(1)}) fusion(f32[2,128,32,64]{1,3,2,0:T(8,128)S(1)} %fusion.49, f32[64,128]{1,0:T(8,128)S(1)} %get-tuple-element.69, f32[64,128]{1,0:T(8,128)S(1)} %get-tuple-element.70, f32[2,128,32,32]{1,0,3,2:T(2,128)} %bitcast.8), kind=kOutput, calls=%fused_computation.4 | convolution fusion | flops 205025280 | bytes 7405568 | tf_op jit(solution)/shard_map/qm,bmjc->bqjc/dot_general | solution.py:14
  68.1 4.6 fusion.8
  72.8 95.4 %all-gather.3.cloned.1.call-done = bf16[1024,4096]{1,0:T(8,128)(2,1)} async-done(((bf16[1024,128]{1,0:T(8,128)(2,1)}), bf16[1024,4096]{1,0:T(8,128)(2,1)}) %all-gather.3.cloned.1.call-update) | async-done | bytes 8388624 | tf_op jit(solution)/shard_map/all_gather | solution.py:130
  168.2 8.2 %multiply_reduce_fusion.3 = (f32[1024]{0:T(1024)}, f32[128,1024]{1,0:T(8,128)}, f32[128,1024]{1,0:T(8,128)}) fusion(f32[3,128,1024]{2,1,0:T(8,128)S(1)} %multiply_add_fusion, bf16[128,4096]{1,0:T(8,128)(2,1)} %all-gather.5.cloned.1.call-done, bf16[1024,4096]{1,0:T(8,128)(2,1)} %all-gather.3.cloned.1.call-done), kind=kOutput, calls=%fused_computation.100 | convolution fusion | flops 1074265088 | bytes 12062720 | tf_op jit(solution)/shard_map/dot_general | solution.py:137
  176.4 1.9 copy.118
  178.3 9.0 %all-to-all-start.2 = ((f32[1,128,1024]{1,0,2:T(1,128)}), f32[1,128,1024]{1,0,2:T(1,128)}, u32[]{:S(2)}, u32[]{:S(2)}) async-start(f32[1,128,1024]{1,0,2:T(1,128)} %copy.118), calls=%async_computation.3 | async-start | bytes 1048576 | tf_op jit(solution)/shard_map/all_to_all | solution.py:69
  187.4 5.0 fusion.6
  192.4 4.7 add_bitcast_fusion.1
  197.1 4.7 subtract_bitcast_fusion.1
  202.1 2.4 convolution_bitcast_fusion
  204.5 2.8 subtract_bitcast_fusion.2
  211.0 1.9 fusion.38
  212.9 4.4 multiply_add_fusion.2
  224.2 2.1 fusion.42
  226.3 3.1 copy.141
  229.9 20.4 %reduce = f32[4096,32]{1,0:T(8,128)} reduce(f32[4096,1,32]{2,1,0:T(1,128)} %bitcast.258, f32[]{:T(128)} %broadcast.311), dimensions={1}, to_apply=%bitcast.226.reduce_sub_computation | reduce | bytes 1048580
  250.3 3.1 reshape.123
  253.4 9.5 %all-to-all-start.1 = ((f32[32,1,4096]{2,1,0:T(1,128)}), f32[32,1,4096]{2,1,0:T(1,128)}, u32[]{:S(2)}, u32[]{:S(2)}) async-start(f32[32,1,4096]{2,1,0:T(1,128)} %reshape.123), calls=%async_computation.1 | async-start | bytes 1048576 | tf_op jit(solution)/shard_map/all_to_all | solution.py:83
  263.2 5.0 fusion.14
  268.3 2.1 fusion.15
  270.4 3.4 fusion.18
  273.8 4.0 all-to-all-done.1
  277.9 3.7 reduce.1
  281.6 5.9 %reshape.124 = f32[4096,1,32]{2,1,0:T(1,128)} reshape(f32[32,4096]{1,0:T(8,128)} %reduce.1) | data formatting | bytes 1048576
  287.6 5.8 %copy.115 = f32[1,4096,32]{1,0,2:T(1,128)} copy(f32[1,4096,32]{2,0,1:T(1,128)} %bitcast.257) | data formatting | bytes 1048576 | tf_op jit(solution)/shard_map/all_to_all | solution.py:83
  293.4 2.2 copy.116
  295.6 2.0 copy.117
  297.6 6.3 %fusion.71 = f32[128,4096]{1,0:T(8,128)} fusion(bf16[1024,4096]{1,0:T(8,128)(2,1)} %all-gather.3.cloned.1.call-done, f32[3,128,1024]{2,1,0:T(8,128)S(1)} %multiply_add_fusion, f32[128,1024]{1,0:T(8,128)} %copy.117, f32[1024]{0:T(1024)S(1)} %copy-done.16), kind=kOutput, calls=%fused_computation.109 | convolution fusion | flops 1074397184 | bytes 12587008 | tf_op jit(solution)/shard_map/dot_general | solution.py:128
  303.9 5.3 subtract_bitcast_fusion
  309.2 2.5 fusion.2
  311.7 3.5 fusion.34
  315.2 4.6 copy.142
  319.8 6.7 %reshape.125 = f32[32,1,8192]{2,1,0:T(1,128)} reshape(f32[4096,2,32]{2,1,0:T(2,128)} %bitcast.255) | data formatting | bytes 2097152
  326.5 33.8 %all_to_all.60 = f32[32,1,8192]{2,1,0:T(1,128)} all-to-all(f32[32,1,8192]{2,1,0:T(1,128)} %reshape.125), channel_id=1, replica_groups=mesh['ctx'=32,'tp'=8] {'ctx'}, dimensions={0} | all-to-all | bytes 2097152 | tf_op jit(solution)/shard_map/all_to_all | solution.py:83
  360.3 5.4 %reduce.2 = f32[32,8192]{1,0:T(8,128)} reduce(f32[32,1,8192]{2,1,0:T(1,128)} %all_to_all.60, f32[]{:T(128)} %broadcast.311), dimensions={1}, to_apply=%all_to_all.53.reduce_sub_computation | reduce | bytes 2097156 | tf_op jit(solution)/shard_map/all_to_all | solution.py:83
  365.7 5.9 %reshape.126 = f32[4096,2,32]{2,1,0:T(2,128)} reshape(f32[32,8192]{1,0:T(8,128)} %reduce.2) | data formatting | bytes 2097152
  371.6 4.6 copy.143
  378.4 2.1 copy.129
  383.4 4.3 collective-permute-start.1
  391.4 1.9 multiply_reduce_fusion.2
  393.3 133.6 %all-reduce = (f32[1024]{0:T(1024)}, f32[3,3,1024]{2,0,1:T(4,128)S(1)}) all-reduce(f32[1024]{0:T(1024)S(1)} %copy-done.17, f32[3,3,1024]{2,0,1:T(4,128)S(1)} %pad_maximum_fusion.13), channel_id=1, replica_groups=mesh['ctx'=32,'tp'=8] {'ctx'}, use_global_device_ids=true, to_apply=%region_2.3 | all-reduce | flops 10240 | bytes 81920 | tf_op jit(solution)/shard_map/psum | solution.py:171
  527.5 2.0 slice_bitcast_fusion.1
  (75 shorter events, 30.6 us)
Async XLA Ops:
  7.2 65.6 %all-gather.5.cloned.1.call-start = ((), (), s32[]{:S(2)}) async-start(), calls=%async_computation.7 | async-start | bytes 1179648 | tf_op jit(solution)/shard_map/all_gather | solution.py:136
  7.9 160.3 %all-gather.3.cloned.1.call-start = ((), (), s32[]{:S(2)}) async-start(), calls=%async_computation.5 | async-start | bytes 8650752 | tf_op jit(solution)/shard_map/all_gather | solution.py:130
  9.4 8.6 %collective-permute-start = (bf16[3,2,1024]{2,1,0:T(2,128)(2,1)S(1)}, bf16[3,2,1024]{2,1,0:T(2,128)(2,1)S(1)}, u32[]{:S(2)}, u32[]{:S(2)}) collective-permute-start(bf16[3,2,1024]{2,1,0:T(2,128)(2,1)S(1)} %pad_maximum_fusion.17), channel_id=1, source_target_pairs={{0,8},{8,16},{16,24},{24,32},{32,40},{40,48},{48,56},{56,64},{64,7... | collective-permute-start | bytes 36872 | tf_op jit(solution)/shard_map/ppermute | solution.py:10
  19.4 1.0 copy-start.15
  23.9 33.7 %all-to-all-start = ((f32[2,128,1024]{1,0,2:T(2,128)}), f32[2,128,1024]{1,0,2:T(2,128)}, u32[]{:S(2)}, u32[]{:S(2)}) async-start(f32[2,128,1024]{1,0,2:T(2,128)} %copy.105), calls=%async_computation | async-start | bytes 2097152 | tf_op jit(solution)/shard_map/all_to_all | solution.py:69
  66.8 1.3 copy-start.1
  178.3 23.8 %all-to-all-start.2 = ((f32[1,128,1024]{1,0,2:T(1,128)}), f32[1,128,1024]{1,0,2:T(1,128)}, u32[]{:S(2)}, u32[]{:S(2)}) async-start(f32[1,128,1024]{1,0,2:T(1,128)} %copy.118), calls=%async_computation.3 | async-start | bytes 1048576 | tf_op jit(solution)/shard_map/all_to_all | solution.py:69
  187.3 5.0 copy-start
  187.3 5.0 copy-start.6
  209.1 3.7 copy-start.14
  211.0 1.9 copy-start.13
  253.4 24.5 %all-to-all-start.1 = ((f32[32,1,4096]{2,1,0:T(1,128)}), f32[32,1,4096]{2,1,0:T(1,128)}, u32[]{:S(2)}, u32[]{:S(2)}) async-start(f32[32,1,4096]{2,1,0:T(1,128)} %reshape.123), calls=%async_computation.1 | async-start | bytes 1048576 | tf_op jit(solution)/shard_map/all_to_all | solution.py:83
  263.0 266.6 %reduce-scatter.2.cloned.1.call-start = ((), (), s32[]{:S(2)}) async-start(), calls=%async_computation.6 | async-start | bytes 2359296 | tf_op jit(solution)/shard_map/reduce_scatter | solution.py:133
  263.2 5.1 copy-start.2
  263.2 5.1 copy-start.3
  268.3 2.2 copy-start.4
  268.3 2.2 copy-start.5
  287.6 10.0 %copy-start.16 = (f32[1024]{0:T(1024)S(1)}, f32[1024]{0:T(1024)}, u32[]{:S(2)}) copy-start(f32[1024]{0:T(1024)} %param.17) | copy-start | bytes 12292
  382.3 6.6 %copy-start.7 = (f32[1,128,1024]{2,1,0:T(8,128)}, f32[1,128,1024]{2,1,0:T(8,128)S(1)}, u32[]{:S(2)}) copy-start(f32[1,128,1024]{2,1,0:T(8,128)S(1)} %get-tuple-element.52) | copy-start | bytes 1572868
  382.3 6.6 %copy-start.9 = (f32[1,128,1024]{2,1,0:T(8,128)}, f32[1,128,1024]{2,1,0:T(8,128)S(1)}, u32[]{:S(2)}) copy-start(f32[1,128,1024]{2,1,0:T(8,128)S(1)} %get-tuple-element.53) | copy-start | bytes 1572868
  382.3 6.6 %copy-start.11 = (f32[1,128,1024]{2,1,0:T(8,128)}, f32[1,128,1024]{2,1,0:T(8,128)S(1)}, u32[]{:S(2)}) copy-start(f32[1,128,1024]{2,1,0:T(8,128)S(1)} %get-tuple-element.58) | copy-start | bytes 1572868
  383.4 6.5 %collective-permute-start.1 = (f32[3,2,1024]{2,1,0:T(2,128)}, f32[3,2,1024]{2,1,0:T(2,128)}, u32[]{:S(2)}, u32[]{:S(2)}) collective-permute-start(f32[3,2,1024]{2,1,0:T(2,128)} %slice.111), channel_id=1, source_target_pairs={{8,0},{16,8},{24,16},{32,24},{40,32},{48,40},{56,48},{64,56},{72,6... | collective-permute-start | bytes 73736 | tf_op jit(solution)/shard_map/ppermute | solution.py:10
  389.0 2.4 copy-start.8
  389.0 2.4 copy-start.10
  389.0 2.4 copy-start.12
  391.4 1.9 copy-start.17
Sparse Core Ops, SparseCore 0:
  9.8 51.8 all-gather.4
  64.2 103.9 all-gather.2
  304.0 65.6 reduce-scatter.1
where the time goes:
time: 549 us; the launch traced here: 538 us
  blocking collectives  167 us (30%)
  waiting for transfers between devices  133 us (24%)
  matrix products  88.8 us (16%)
  local copies, waits for them, and re-layouts  60.4 us (11%)
  other arithmetic  41.4 us (8%)
  starting transfers between devices  32.9 us (6%)
  between operations  14.7 us (3%)
    psum x1, blocking collectives, local(): grad_skip, grad_short = lax.psum((skip_term, tap_terms), 'ctx')  134 us
    all_gather x1, waiting for transfers between devices, local(): lax.all_gather(out_weight, 'ctx', axis=1, tiled=True)  95.4 us
    dot_general x24, matrix products, mixer(): return jnp.einsum(form, left, right, precision=lax.Precision.HIGHEST)  74.3 us
    all_to_all x1, blocking collectives, signal_channels(): lax.all_to_all(joined, 'ctx', split_axis=1, concat_axis=2, tiled=True)  33.8 us
    all_to_all x2, waiting for transfers between devices, spectrum_channels(): lax.all_to_all(field, 'ctx', split_axis=2, concat_axis=1, tiled=True)  26 us
    unnamed x45, local copies, waits for them, and re-layouts  25.6 us
    unnamed x1, other arithmetic  20.4 us
    all_to_all x2, starting transfers between devices, spectrum_channels(): lax.all_to_all(field, 'ctx', split_axis=2, concat_axis=1, tiled=True)  16.8 us
  transfers between devices with their start and end apart: 8, of which 5 were waited for; matrix products, arithmetic and copies ran while one was open for 19% of the time, Pallas kernels for 0%

commit v1 on v0

v1 whole, which is shorter than its diff:
```python
import jax
import jax.numpy as jnp
import ml_dtypes
import numpy as np
from jax import lax
from jax.experimental import pallas as pl
from jax.experimental.pallas import tpu as pltpu
from jax.sharding import PartitionSpec as P

F32 = jnp.float32
BF16 = jnp.bfloat16
GROUP = 16
FILTER, GATED, MIXING, GRAD_MIX, GRAD_GATED, GRAD_FILTER = range(6)


def halves(matrix):
    high = matrix.astype(np.float32).astype(ml_dtypes.bfloat16)
    low = (matrix - high.astype(np.float64)).astype(np.float32).astype(ml_dtypes.bfloat16)
    return np.stack([high, low])


def tables(n, seq):
    total = 2 * n * seq
    q = np.arange(n + 1)
    m = np.arange(n)
    theta = 2 * np.pi * ((q[:, None] * m[None, :]) % (2 * n)) / (2 * n)
    forward = np.concatenate([np.cos(theta), -np.sin(theta)[1:n]])
    weight = np.where((q == 0) | (q == n), 1.0, 2.0)[:, None] / total
    back = np.concatenate([weight * np.cos(theta), (-weight * np.sin(theta))[1:n]]).T
    eye = np.eye(GROUP)
    j = np.arange(seq)
    phi = 2 * np.pi * ((j[:, None] * j[None, :]) % seq) / seq
    c, s = np.cos(phi), np.sin(phi)
    inner = np.block([[c, -s], [s, c]])
    inner_back = np.block([[c, s], [-s, c]])
    turn = 2 * np.pi * (q[:, None] * j[None, :]) / total
    twiddle = np.stack([np.cos(turn), np.sin(turn)]).astype(np.float32)
    twiddle = np.repeat(twiddle, GROUP, axis=1)
    return (
        halves(np.kron(forward, eye)),
        halves(np.kron(back, eye)),
        halves(np.stack([inner, inner_back])),
        twiddle,
    )


def split(value):
    high = value.astype(BF16)
    return high, (value - high.astype(F32)).astype(BF16)


def mm(left, right):
    return jnp.dot(left, right, preferred_element_type=F32)


def body(n, nz, ny, refs):
    (
        query, key, value, tap_q, tap_k, tap_v, filt, skip, weight, cot,
        outer_hbm, outer_back_hbm, inner_hbm, twiddle_hbm,
        mixed_out, out_q, out_k, out_v, out_filter, out_skip, out_short,
        outer, outer_back, inner, twiddle,
        halo, ext, short, gated, mixing, grad_hidden, grad_mix, gext,
        sent, got, wide, cots, part, part_b, core_got, chip_sent, chip_got, hid,
        rows_b, rows_got, pair_sent, pair_got, final_b,
        spec_u, spec_h, spec_d, stage, tails, tails_got, tails_sum,
        const_sem, a2a_send, a2a_recv, send, recv,
    ) = refs
    seq, ch = query.shape
    half = ch // 2
    rows = 16 * n
    q_rows = GROUP * (n + 1)
    me = lax.axis_index("ctx")
    tp = lax.axis_index("tp")
    z, b = lax.div(me, 4), lax.rem(me, 4)
    xh, core = lax.div(b, 2), lax.rem(b, 2)
    y, xl = lax.div(tp, 2), lax.rem(tp, 2)
    counter = [0]
    pending = []

    def remote(src, dst, ctx, t):
        k = counter[0]
        counter[0] += 1
        copy = pltpu.make_async_remote_copy(
            src_ref=src, dst_ref=dst, send_sem=send.at[k], recv_sem=recv.at[k],
            device_id=(ctx, t), device_id_type=pl.DeviceIdType.MESH,
        )
        copy.start()
        pending.append(copy)
        return copy

    def at16(index):
        return pl.ds(pl.multiple_of(index * 16, 16), 16)

    def lanes(index, size=128):
        return pl.ds(pl.multiple_of(index * size, 128), size)

    def block(index, size=None):
        size = seq if size is None else size
        return pl.ds(pl.multiple_of(index * size, size), size)

    def spread(k):
        def step(r, carry):
            dst = lax.rem(me + r, n)
            pltpu.make_async_remote_copy(
                src_ref=sent.at[k, at16(dst)], dst_ref=got.at[k, at16(me)],
                send_sem=a2a_send.at[k], recv_sem=a2a_recv.at[k],
                device_id=(dst, tp), device_id_type=pl.DeviceIdType.MESH,
            ).start()
            return carry

        lax.fori_loop(1, n, step, 0)
        got[k, at16(me), :] = sent[k, at16(me), :]

    def arrive(k):
        whole = got.at[k, pl.ds(0, rows - 16)]
        pltpu.make_async_copy(whole, whole, a2a_recv.at[k]).wait()

    def left(k):
        whole = sent.at[k, pl.ds(0, rows - 16)]
        pltpu.make_async_copy(whole, whole, a2a_send.at[k]).wait()

    def to_channels(x, k):
        for g in range(2):
            sent[k, :, g * seq : (g + 1) * seq] = x[:, g * half : (g + 1) * half].T.astype(BF16)

    def to_tokens(k):
        return jnp.concatenate(
            [got[k, :, g * seq : (g + 1) * seq].astype(F32).T for g in range(2)], axis=1
        )

    def forward(k, spec):
        u = got[k]
        stage[...] = mm(outer[0], u) + mm(outer[1], u)
        cos, sin = twiddle[0], twiddle[1]
        zero = jnp.zeros((GROUP, seq), F32)
        for g in range(2):
            cols = pl.ds(g * seq, seq)
            real = stage[:q_rows, cols]
            imag = jnp.concatenate([zero, stage[q_rows:, cols], zero])
            pair = jnp.concatenate([real * cos + imag * sin, imag * cos - real * sin], axis=1)
            high, low = split(pair)
            spec[g] = mm(high, inner[0, 0]) + mm(low, inner[0, 0]) + mm(high, inner[1, 0])

    def product(first, second, g, conj):
        ar, ai = first[g, :, :seq], first[g, :, seq:]
        br, bi = second[g, :, :seq], second[g, :, seq:]
        if conj:
            return jnp.concatenate([ar * br + ai * bi, ar * bi - ai * br], axis=1)
        return jnp.concatenate([ar * br - ai * bi, ar * bi + ai * br], axis=1)

    def inverse(first, second, conj, k):
        cos, sin = twiddle[0], twiddle[1]
        for g in range(2):
            high, low = split(product(first, second, g, conj))
            turned = mm(high, inner[0, 1]) + mm(low, inner[0, 1]) + mm(high, inner[1, 1])
            real, imag = turned[:, :seq], turned[:, seq:]
            cols = pl.ds(g * seq, seq)
            stage[:q_rows, cols] = real * cos - imag * sin
            stage[q_rows:, cols] = (imag * cos + real * sin)[GROUP : q_rows - GROUP]
        high, low = split(stage[...])
        result = mm(outer_back[0], high) + mm(outer_back[0], low) + mm(outer_back[1], high)
        sent[k] = result.astype(BF16)

    barrier = pltpu.get_barrier_semaphore()

    def greet(r, carry):
        pl.semaphore_signal(
            barrier, inc=1, device_id=(lax.rem(me + r, n), tp),
            device_id_type=pl.DeviceIdType.MESH,
        )
        return carry

    lax.fori_loop(1, n, greet, 0)
    others = [(y, 1 - xl)] + [(lax.rem(y + r, ny), xl) for r in range(1, ny)]
    for oy, ox in others:
        pl.semaphore_signal(
            barrier, inc=1, device_id=(me, oy * 2 + ox), device_id_type=pl.DeviceIdType.MESH
        )
    consts = [
        pltpu.make_async_copy(src, dst, const_sem.at[i])
        for i, (src, dst) in enumerate(
            [(outer_hbm, outer), (inner_hbm, inner), (twiddle_hbm, twiddle), (outer_back_hbm, outer_back)]
        )
    ]
    for copy in consts:
        copy.start()
    to_channels(filt[...], FILTER)
    wide[:, lanes(z)] = weight[...]
    cots[block(b), lanes(tp)] = cot[:, lanes(b)]
    tails[...] = jnp.zeros_like(tails)
    pl.semaphore_wait(barrier, n - 1 + len(others))

    following, preceding = lax.rem(me + 1, n), lax.rem(me + n - 1, n)
    halos = [
        remote(x.at[pl.ds(seq - 16, 16)], halo.at[i], following, tp)
        for i, x in enumerate((query, key, value))
    ]

    full = nz // 2 - 1
    up, down = lax.rem(z + 1, nz) * 4 + b, lax.rem(z + nz - 1, nz) * 4 + b

    def ring(s):
        if s < full:
            part_up = part_down = pl.ds(0, ch)
        else:
            part_up, part_down = pl.ds(0, half), pl.ds(half, half)
        slot_up, slot_down = lanes(lax.rem(z + nz - s, nz)), lanes(lax.rem(z + s, nz))
        if s == 0:
            src_up, src_down = weight.at[part_up], weight.at[part_down]
        else:
            src_up, src_down = wide.at[part_up, slot_up], wide.at[part_down, slot_down]
        return (
            remote(src_up, wide.at[part_up, slot_up], up, tp),
            remote(src_down, wide.at[part_down, slot_down], down, tp),
        )

    def landed(copies):
        for copy in copies:
            copy.wait_recv()

    def mate(r):
        other = lax.rem(b + r, 4)
        return other, z * 4 + other

    hop = ring(0)
    cot_first = []
    for r in range(1, 4):
        other, ctx = mate(r)
        cot_first.append(remote(cot.at[:, lanes(other)], cots.at[block(b), lanes(tp)], ctx, tp))
    spread(FILTER)

    landed(halos)
    taps = (tap_q, tap_k, tap_v)
    for i, x in enumerate((query, key, value)):
        ext[i, :8] = jnp.where(me == 0, 0.0, halo[i, 8:16].astype(F32))
        ext[i, 8:] = x[...].astype(F32)
        short[i] = (
            taps[i][0:1] * ext[i, pl.ds(8, seq)]
            + taps[i][1:2] * ext[i, pl.ds(7, seq)]
            + taps[i][2:3] * ext[i, pl.ds(6, seq)]
        )
    gated[...] = short[1] * short[2]
    to_channels(gated[...], GATED)
    spread(GATED)

    landed(cot_first)
    cot_pair = remote(cots.at[:, lanes(tp)], cots.at[:, lanes(tp)], me, y * 2 + 1 - xl)
    if full > 0:
        landed(hop)
        hop = ring(1)
    cot_pair.wait_recv()
    cot_last = []
    for oy, ox in others[1:]:
        cot_last.append(remote(cots.at[:, lanes(y, 256)], cots.at[:, lanes(y, 256)], me, oy * 2 + ox))

    for copy in consts:
        copy.wait()
    arrive(FILTER)
    forward(FILTER, spec_h)
    if full > 1:
        landed(hop)
        hop = ring(2)
    arrive(GATED)
    forward(GATED, spec_u)
    if full > 2:
        landed(hop)
        hop = ring(3)
    inverse(spec_h, spec_u, False, MIXING)
    spread(MIXING)

    landed(hop)
    landed(cot_last)

    def grad_columns(i, carry):
        part[:, lanes(i, 256)] = lax.dot_general(
            cots[...], wide[block(i, 256), :], (((1,), (1,)), ((), ())), preferred_element_type=F32
        )
        part_b[:, lanes(i, 256)] = part[:, lanes(i, 256)].astype(BF16)
        return carry

    lax.fori_loop(0, ch // 256, grad_columns, 0)
    sibling = z * 4 + xh * 2 + 1 - core
    twin = z * 4 + (1 - xh) * 2 + core
    core_copies = [
        remote(part_b.at[block(i * 2 + 1 - core)], core_got.at[i], sibling, tp) for i in range(2)
    ]

    arrive(MIXING)
    mixing[...] = to_tokens(MIXING) + skip[...] * gated[...]
    hid[block(b), :] = (short[0] * mixing[...]).astype(BF16)

    landed(core_copies)
    chip_sent[...] = (part[block((1 - xh) * 2 + core), :] + core_got[1 - xh].astype(F32)).astype(BF16)
    chip_copy = remote(chip_sent, chip_got, twin, tp)
    hid_twin = remote(hid.at[block(b)], hid.at[block(b)], twin, tp)
    hid_sib = remote(hid.at[block(b)], hid.at[block(b)], sibling, tp)

    chip_copy.wait_recv()
    grad_hidden[...] = (
        part[block(b), :] + core_got[xh].astype(F32) + chip_got[...].astype(F32)
    )
    grad_mix[...] = grad_hidden[...] * short[0]
    to_channels(grad_mix[...], GRAD_MIX)
    spread(GRAD_MIX)

    hid_twin.wait_recv()
    other_b = (1 - xh) * 2 + core
    hid_far = remote(hid.at[block(other_b)], hid.at[block(other_b)], sibling, tp)
    gext[0, :seq] = grad_hidden[...] * mixing[...]
    halo_q = remote(gext.at[0, pl.ds(0, 8)], gext.at[0, pl.ds(seq, 8)], preceding, tp)

    def tap_sums(i):
        grads = gext[i, :seq]
        for o in range(3):
            tails[8 * i + o, :] = jnp.sum(grads * ext[i, pl.ds(8 - o, seq)], axis=0)

    tap_sums(0)
    tails[24, :] = jnp.sum(grad_mix[...] * gated[...], axis=0)

    hid_sib.wait_recv()
    hid_far.wait_recv()

    def out_columns(i, carry):
        part[:, lanes(i, 256)] = mm(hid[...], wide[:, lanes(i, 256)])
        rows_b[:, lanes(i, 256)] = part[:, lanes(i, 256)].astype(BF16)
        return carry

    lax.fori_loop(0, wide.shape[1] // 256, out_columns, 0)
    rows_copies = [
        remote(rows_b.at[:, lanes(oy, 256)], rows_got.at[r], me, oy * 2 + ox)
        for r, (oy, ox) in enumerate(others[1:])
    ]

    arrive(GRAD_MIX)
    forward(GRAD_MIX, spec_d)
    inverse(spec_h, spec_d, True, GRAD_GATED)
    spread(GRAD_GATED)

    landed(rows_copies)
    total = part[:, lanes(y, 256)]
    for r in range(len(rows_copies)):
        total += rows_got[r].astype(F32)
    part[:, lanes(y, 256)] = total
    pair_sent[...] = part[:, lanes(y * 2 + 1 - xl)]
    pair_copy = remote(pair_sent, pair_got, me, y * 2 + 1 - xl)

    inverse(spec_u, spec_d, True, GRAD_FILTER)
    spread(GRAD_FILTER)

    pair_copy.wait_recv()
    final_b[...] = (part[:, lanes(tp)] + pair_got[...]).astype(BF16)
    mixed_out[:, lanes(b)] = final_b[block(b), :]
    final_copies = []
    for r in range(1, 4):
        other, ctx = mate(r)
        final_copies.append(remote(final_b.at[block(other)], mixed_out.at[:, lanes(b)], ctx, tp))

    def returned(i, out):
        gext[i, seq:] = jnp.where(me == n - 1, 0.0, gext[i, seq:])
        out[...] = (
            taps[i][0:1] * gext[i, pl.ds(0, seq)]
            + taps[i][1:2] * gext[i, pl.ds(1, seq)]
            + taps[i][2:3] * gext[i, pl.ds(2, seq)]
        ).astype(BF16)

    halo_q.wait_recv()
    returned(0, out_q)

    arrive(GRAD_GATED)
    grad = to_tokens(GRAD_GATED) + skip[...] * grad_mix[...]
    gext[1, :seq] = grad * short[2]
    gext[2, :seq] = grad * short[1]
    halo_kv = [
        remote(gext.at[i, pl.ds(0, 8)], gext.at[i, pl.ds(seq, 8)], preceding, tp) for i in (1, 2)
    ]
    tap_sums(1)
    tap_sums(2)

    across = ch // 128

    def tile(ref, d):
        return ref.at[block(lax.div(d, across), 8), lanes(lax.rem(d, across))]

    def hand_in(r, carry):
        dst = lax.rem(me + r, n)
        pltpu.make_async_remote_copy(
            src_ref=tile(tails, dst), dst_ref=tails_got.at[block(me, 8)],
            send_sem=a2a_send.at[6], recv_sem=a2a_recv.at[6],
            device_id=(dst, tp), device_id_type=pl.DeviceIdType.MESH,
        ).start()
        return carry

    def hand_out(r, carry):
        dst = lax.rem(me + r, n)
        pltpu.make_async_remote_copy(
            src_ref=tile(tails_sum, me), dst_ref=tile(tails_sum, me),
            send_sem=a2a_send.at[7], recv_sem=a2a_recv.at[7],
            device_id=(dst, tp), device_id_type=pl.DeviceIdType.MESH,
        ).start()
        return carry

    def tails_wait(sem):
        whole = tails_got.at[pl.ds(0, 8 * (n - 1))]
        pltpu.make_async_copy(whole, whole, sem).wait()

    mine = (block(lax.div(me, across), 8), lanes(lax.rem(me, across)))
    lax.fori_loop(1, n, hand_in, 0)
    tails_got[block(me, 8), :] = tails[mine]
    tails_wait(a2a_recv.at[6])
    tails_sum[mine] = jnp.sum(tails_got[...].reshape(n, 8, 128), axis=0)
    lax.fori_loop(1, n, hand_out, 0)

    landed(halo_kv)
    returned(1, out_k)
    returned(2, out_v)
    arrive(GRAD_FILTER)
    out_filter[...] = to_tokens(GRAD_FILTER).astype(BF16)

    tails_wait(a2a_recv.at[7])
    for i in range(3):
        out_short[i] = tails_sum[8 * i : 8 * i + 3, :]
    out_skip[...] = tails_sum[24:25, :]
    landed(final_copies)
    for copy in pending:
        copy.wait_send()
    for k in range(6):
        left(k)
    tails_wait(a2a_send.at[6])
    tails_wait(a2a_send.at[7])


def local(*args):
    n, tp = lax.axis_size("ctx"), lax.axis_size("tp")
    nz, ny = n // 4, tp // 2
    query, key, value, tap_q, tap_k, tap_v, filt, skip, weight, cot = args
    seq, ch = query.shape
    consts = [jnp.asarray(t) for t in tables(n, seq)]
    outer, outer_back, inner, twiddle = consts
    q_rows = GROUP * (n + 1)
    d_cols = nz * 128
    tokens4 = 4 * seq

    def vmem(shape, dtype=F32):
        return pltpu.VMEM(shape, dtype)

    scratch = [
        vmem(outer.shape, BF16), vmem(outer_back.shape, BF16), vmem(inner.shape, BF16),
        vmem(twiddle.shape),
        vmem((3, 16, ch), BF16), vmem((3, seq + 8, ch)), vmem((3, seq, ch)),
        vmem((seq, ch)), vmem((seq, ch)), vmem((seq, ch)), vmem((seq, ch)),
        vmem((3, seq + 8, ch)),
        vmem((6, 16 * n, 2 * seq), BF16), vmem((6, 16 * n, 2 * seq), BF16),
        vmem((ch, d_cols), BF16), vmem((tokens4, d_cols), BF16),
        vmem((tokens4, max(ch, d_cols))), vmem((tokens4, ch), BF16),
        vmem((2, seq, ch), BF16), vmem((seq, ch), BF16), vmem((seq, ch), BF16),
        vmem((tokens4, ch), BF16),
        vmem((tokens4, d_cols), BF16), vmem((max(ny - 1, 1), tokens4, 256), BF16),
        vmem((tokens4, 128)), vmem((tokens4, 128)), vmem((tokens4, 128), BF16),
        vmem((2, q_rows, 2 * seq)), vmem((2, q_rows, 2 * seq)), vmem((2, q_rows, 2 * seq)),
        vmem((2 * n * GROUP, 2 * seq)),
        vmem((32, ch)), vmem((8 * n, 128)), vmem((32, ch)),
        pltpu.SemaphoreType.DMA((4,)),
        pltpu.SemaphoreType.DMA((8,)), pltpu.SemaphoreType.DMA((8,)),
        pltpu.SemaphoreType.DMA((48,)), pltpu.SemaphoreType.DMA((48,)),
    ]
    shape = jax.ShapeDtypeStruct
    inside = pl.BlockSpec(memory_space=pltpu.VMEM)
    outside = pl.BlockSpec(memory_space=pl.ANY)
    out_shape = (
        shape(cot.shape, BF16),
        shape((seq, ch), BF16), shape((seq, ch), BF16), shape((seq, ch), BF16),
        shape((seq, ch), BF16),
        shape((1, ch), F32), shape((3, 3, ch), F32),
    )
    results = pl.pallas_call(
        lambda *refs: body(n, nz, ny, refs),
        out_shape=out_shape,
        in_specs=[inside] * 10 + [outside] * 4,
        out_specs=[inside] * 7,
        scratch_shapes=scratch,
        compiler_params=pltpu.CompilerParams(
            collective_id=0, has_side_effects=True, vmem_limit_bytes=60 * 1024 * 1024
        ),
        name="hyena",
    )(query, key, value, tap_q, tap_k, tap_v, filt, skip.reshape(1, ch), weight, cot, *consts)
    return results[:5] + (results[5].reshape(ch), results[6])


def solution(mesh):
    in_specs = (
        P("ctx", "tp"),
        P("ctx", "tp"),
        P("ctx", "tp"),
        P(None, "tp"),
        P(None, "tp"),
        P(None, "tp"),
        P("ctx", "tp"),
        P("tp"),
        P("tp", "ctx"),
        P("ctx", "tp"),
    )
    out_specs = (
        P("ctx", "tp"),
        P("ctx", "tp"),
        P("ctx", "tp"),
        P("ctx", "tp"),
        P("ctx", "tp"),
        P("tp"),
        P(None, None, "tp"),
    )
    return jax.shard_map(local, mesh=mesh, in_specs=in_specs, out_specs=out_specs, check_vma=False)
```

time: 549 us -> 128 us (0.23)
  the two profiles are of different devices: /device:TPU:128 before, /device:TPU:1 now
where the time goes in v1:
time: 128 us
  Pallas kernels  118 us (92%)
  local copies, waits for them, and re-layouts  9.48 us (7%)
    pallas_call x1, Pallas kernels, local(): pl.pallas_call(lambda *refs: body(n, nz, ny, refs), out_shape=out_shape,...  118 us
    unnamed x11, local copies, waits for them, and re-layouts  9.48 us

profile of v1, /device:TPU:1, one launch (start us, length us, event | category | flops | bytes accessed | tf_op | source)
XLA Modules:
  0.0 127.9 jit_solution(9836119950123052040)
XLA Ops:
  0.6 117.8 %hyena.1 = (bf16[128,512]{1,0:T(8,128)(2,1)}, bf16[128,1024]{1,0:T(8,128)(2,1)}, bf16[128,1024]{1,0:T(8,128)(2,1)}, bf16[128,1024]{1,0:T(8,128)(2,1)}, bf16[128,...) custom-call(bf16[128,1024]{1,0:T(8,128)(2,1)} %refs_0_.1, bf16[128,1024]{1,0:T(8,128)(2,1)} %refs_1_.1, ...), custom_call_target="tpu_custom_call" | custom-call | tf_op jit(solution)/shard_map/hyena/pallas_call | solution.py:475
  118.4 0.0 copy-start.1
  118.4 0.0 copy-start
  118.4 1.6 %copy.28 = bf16[128,512]{1,0:T(8,128)(2,1)} copy(bf16[128,512]{1,0:T(8,128)(2,1)} %get-tuple-element.28) | data formatting | bytes 262144
  120.0 1.7 %copy.29 = bf16[128,1024]{1,0:T(8,128)(2,1)} copy(bf16[128,1024]{1,0:T(8,128)(2,1)} %get-tuple-element.29) | data formatting | bytes 524288
  121.7 1.7 %copy.30 = bf16[128,1024]{1,0:T(8,128)(2,1)} copy(bf16[128,1024]{1,0:T(8,128)(2,1)} %get-tuple-element.30) | data formatting | bytes 524288
  123.4 1.7 %copy.31 = bf16[128,1024]{1,0:T(8,128)(2,1)} copy(bf16[128,1024]{1,0:T(8,128)(2,1)} %get-tuple-element.31) | data formatting | bytes 524288
  125.0 1.7 %copy.32 = bf16[128,1024]{1,0:T(8,128)(2,1)} copy(bf16[128,1024]{1,0:T(8,128)(2,1)} %get-tuple-element.32) | data formatting | bytes 524288
  126.7 0.0 copy-done.1
  126.7 0.6 copy.33
  127.3 0.0 copy-done
  127.3 0.6 copy.34
Async XLA Ops:
  118.4 8.3 %copy-start.1 = (f32[1,1024]{1,0:T(1,128)S(1)}, f32[1,1024]{1,0:T(1,128)}, u32[]{:S(2)}) copy-start(f32[1,1024]{1,0:T(1,128)} %get-tuple-element.19) | copy-start | bytes 12292
  118.4 8.9 %copy-start = (f32[3,3,1024]{2,1,0:T(4,128)S(1)}, f32[3,3,1024]{2,1,0:T(4,128)}, u32[]{:S(2)}) copy-start(f32[3,3,1024]{2,1,0:T(4,128)} %get-tuple-element.34) | copy-start | bytes 110596

commit v2 on v1

--- a/solution.py
+++ b/solution.py
@@ -55,15 +55,17 @@
 
 def body(n, nz, ny, refs):
     (
-        query, key, value, tap_q, tap_k, tap_v, filt, skip, weight, cot,
+        query_hbm, key_hbm, value_hbm, tap_q, tap_k, tap_v, filt_hbm, skip, weight, cot,
         outer_hbm, outer_back_hbm, inner_hbm, twiddle_hbm,
-        mixed_out, out_q, out_k, out_v, out_filter, out_skip, out_short,
+        mixed_hbm, grad_q_hbm, grad_k_hbm, grad_v_hbm, filter_hbm, skip_hbm, short_hbm,
+        query, key, value, filt,
+        mixed_out, out_grads, out_filter, out_skip, out_short,
         outer, outer_back, inner, twiddle,
         halo, ext, short, gated, mixing, grad_hidden, grad_mix, gext,
         sent, got, wide, cots, part, part_b, core_got, chip_sent, chip_got, hid,
         rows_b, rows_got, pair_sent, pair_got, final_b,
         spec_u, spec_h, spec_d, stage, tails, tails_got, tails_sum,
-        const_sem, a2a_send, a2a_recv, send, recv,
+        const_sem, in_sem, out_sem, a2a_send, a2a_recv, send, recv,
     ) = refs
     seq, ch = query.shape
     half = ch // 2
@@ -98,30 +100,38 @@
         size = seq if size is None else size
         return pl.ds(pl.multiple_of(index * size, size), size)
 
-    def spread(k):
+    def spread(k, g=None):
+        cols = pl.ds(0, 2 * seq) if g is None else pl.ds(g * seq, seq)
+        sem = k if g is None else 8 + g
+
         def step(r, carry):
             dst = lax.rem(me + r, n)
             pltpu.make_async_remote_copy(
-                src_ref=sent.at[k, at16(dst)], dst_ref=got.at[k, at16(me)],
-                send_sem=a2a_send.at[k], recv_sem=a2a_recv.at[k],
+                src_ref=sent.at[k, at16(dst), cols], dst_ref=got.at[k, at16(me), cols],
+                send_sem=a2a_send.at[sem], recv_sem=a2a_recv.at[sem],
                 device_id=(dst, tp), device_id_type=pl.DeviceIdType.MESH,
             ).start()
             return carry
 
         lax.fori_loop(1, n, step, 0)
-        got[k, at16(me), :] = sent[k, at16(me), :]
-
-    def arrive(k):
-        whole = got.at[k, pl.ds(0, rows - 16)]
-        pltpu.make_async_copy(whole, whole, a2a_recv.at[k]).wait()
-
-    def left(k):
-        whole = sent.at[k, pl.ds(0, rows - 16)]
-        pltpu.make_async_copy(whole, whole, a2a_send.at[k]).wait()
+        got[k, at16(me), cols] = sent[k, at16(me), cols]
+
+    def arrive(k, g=None):
+        cols = pl.ds(0, 2 * seq) if g is None else pl.ds(g * seq, seq)
+        whole = got.at[k, pl.ds(0, rows - 16), cols]
+        pltpu.make_async_copy(whole, whole, a2a_recv.at[k if g is None else 8 + g]).wait()
+
+    def left(k, g=None):
+        cols = pl.ds(0, 2 * seq) if g is None else pl.ds(g * seq, seq)
+        whole = sent.at[k, pl.ds(0, rows - 16), cols]
+        pltpu.make_async_copy(whole, whole, a2a_send.at[k if g is None else 8 + g]).wait()
+
+    def half_to_channels(x, k, g):
+        sent[k, :, g * seq : (g + 1) * seq] = x.T.astype(BF16)
 
     def to_channels(x, k):
         for g in range(2):
-            sent[k, :, g * seq : (g + 1) * seq] = x[:, g * half : (g + 1) * half].T.astype(BF16)
+            half_to_channels(x[:, g * half : (g + 1) * half], k, g)
 
     def to_tokens(k):
         return jnp.concatenate(
@@ -176,6 +186,18 @@
         pl.semaphore_signal(
             barrier, inc=1, device_id=(me, oy * 2 + ox), device_id_type=pl.DeviceIdType.MESH
         )
+    loads = [
+        pltpu.make_async_copy(src, dst, in_sem.at[i])
+        for i, (src, dst) in enumerate(
+            [
+                (filt_hbm, filt), (weight, wide.at[:, lanes(z)]),
+                (cot.at[:, lanes(b)], cots.at[block(b), lanes(tp)]),
+                (query_hbm, query), (key_hbm, key), (value_hbm, value),
+            ]
+        )
+    ]
+    for copy in loads:
+        copy.start()
     consts = [
         pltpu.make_async_copy(src, dst, const_sem.at[i])
         for i, (src, dst) in enumerate(
@@ -184,35 +206,31 @@
     ]
     for copy in consts:
         copy.start()
+    tails[...] = jnp.zeros_like(tails)
+    loads[0].wait()
     to_channels(filt[...], FILTER)
-    wide[:, lanes(z)] = weight[...]
-    cots[block(b), lanes(tp)] = cot[:, lanes(b)]
-    tails[...] = jnp.zeros_like(tails)
     pl.semaphore_wait(barrier, n - 1 + len(others))
 
     following, preceding = lax.rem(me + 1, n), lax.rem(me + n - 1, n)
     halos = [
         remote(x.at[pl.ds(seq - 16, 16)], halo.at[i], following, tp)
-        for i, x in enumerate((query, key, value))
+        for i, x in enumerate((query_hbm, key_hbm, value_hbm))
     ]
 
     full = nz // 2 - 1
     up, down = lax.rem(z + 1, nz) * 4 + b, lax.rem(z + nz - 1, nz) * 4 + b
 
-    def ring(s):
-        if s < full:
-            part_up = part_down = pl.ds(0, ch)
-        else:
-            part_up, part_down = pl.ds(0, half), pl.ds(half, half)
+    def ring(s, c):
+        piece = pl.ds(c * half, half)
         slot_up, slot_down = lanes(lax.rem(z + nz - s, nz)), lanes(lax.rem(z + s, nz))
-        if s == 0:
-            src_up, src_down = weight.at[part_up], weight.at[part_down]
-        else:
-            src_up, src_down = wide.at[part_up, slot_up], wide.at[part_down, slot_down]
-        return (
-            remote(src_up, wide.at[part_up, slot_up], up, tp),
-            remote(src_down, wide.at[part_down, slot_down], down, tp),
-        )
+        copies = []
+        if s < full or c == 0:
+            src = weight.at[piece] if s == 0 else wide.at[piece, slot_up]
+            copies.append(remote(src, wide.at[piece, slot_up], up, tp))
+        if s < full or c == 1:
+            src = weight.at[piece] if s == 0 else wide.at[piece, slot_down]
+            copies.append(remote(src, wide.at[piece, slot_down], down, tp))
+        return copies
 
     def landed(copies):
         for copy in copies:
@@ -222,13 +240,21 @@
         other = lax.rem(b + r, 4)
         return other, z * 4 + other
 
-    hop = ring(0)
+    hops = [ring(0, c) for c in range(2)]
+
+    def advance(s):
+        for c in range(2):
+            landed(hops[c])
+            hops[c] = ring(s, c) if s <= full else []
+
     cot_first = []
     for r in range(1, 4):
         other, ctx = mate(r)
         cot_first.append(remote(cot.at[:, lanes(other)], cots.at[block(b), lanes(tp)], ctx, tp))
     spread(FILTER)
 
+    for copy in loads[1:]:
+        copy.wait()
     landed(halos)
     taps = (tap_q, tap_k, tap_v)
     for i, x in enumerate((query, key, value)):
@@ -241,73 +267,108 @@
         )
     gated[...] = short[1] * short[2]
     to_channels(gated[...], GATED)
-    spread(GATED)
 
     landed(cot_first)
     cot_pair = remote(cots.at[:, lanes(tp)], cots.at[:, lanes(tp)], me, y * 2 + 1 - xl)
-    if full > 0:
-        landed(hop)
-        hop = ring(1)
-    cot_pair.wait_recv()
-    cot_last = []
-    for oy, ox in others[1:]:
-        cot_last.append(remote(cots.at[:, lanes(y, 256)], cots.at[:, lanes(y, 256)], me, oy * 2 + ox))
+    for s in range(1, full):
+        advance(s)
+        if s == 1:
+            cot_pair.wait_recv()
+            cot_last = [
+                remote(cots.at[:, lanes(y, 256)], cots.at[:, lanes(y, 256)], me, oy * 2 + ox)
+                for oy, ox in others[1:]
+            ]
+    if full < 2:
+        cot_pair.wait_recv()
+        cot_last = [
+            remote(cots.at[:, lanes(y, 256)], cots.at[:, lanes(y, 256)], me, oy * 2 + ox)
+            for oy, ox in others[1:]
+        ]
 
     for copy in consts:
         copy.wait()
     arrive(FILTER)
     forward(FILTER, spec_h)
-    if full > 1:
-        landed(hop)
-        hop = ring(2)
+    if full > 0:
+        advance(full)
+    spread(GATED)
+
+    advance(full + 1)
+    landed(cot_last)
+    sibling = z * 4 + xh * 2 + 1 - core
+    twin = z * 4 + (1 - xh) * 2 + core
+    far = (1 - xh) * 2 + core
+    core_copies = []
+    for g in range(2):
+        cols = pl.ds(g * half, half)
+        for lo in range(g * half, (g + 1) * half, 256) if half >= 256 else [g * half]:
+            some = pl.ds(lo, min(256, half))
+            part[:, some] = lax.dot_general(
+                cots[...], wide[some, :], (((1,), (1,)), ((), ())), preferred_element_type=F32
+            )
+        for i in range(2):
+            theirs = block(i * 2 + 1 - core)
+            part_b[theirs, cols] = part[theirs, cols].astype(BF16)
+        core_copies.append(
+            [remote(part_b.at[block(i * 2 + 1 - core), cols], core_got.at[g, i], sibling, tp) for i in range(2)]
+        )
+    chip_copies = []
+    for g in range(2):
+        cols = pl.ds(g * half, half)
+        landed(core_copies[g])
+        chip_sent[g] = (part[block(far), cols] + core_got[g, 1 - xh].astype(F32)).astype(BF16)
+        chip_copies.append(remote(chip_sent.at[g], chip_got.at[g], twin, tp))
+
     arrive(GATED)
     forward(GATED, spec_u)
-    if full > 2:
-        landed(hop)
-        hop = ring(3)
     inverse(spec_h, spec_u, False, MIXING)
     spread(MIXING)
 
-    landed(hop)
-    landed(cot_last)
-
-    def grad_columns(i, carry):
-        part[:, lanes(i, 256)] = lax.dot_general(
-            cots[...], wide[block(i, 256), :], (((1,), (1,)), ((), ())), preferred_element_type=F32
-        )
-        part_b[:, lanes(i, 256)] = part[:, lanes(i, 256)].astype(BF16)
-        return carry
-
-    lax.fori_loop(0, ch // 256, grad_columns, 0)
-    sibling = z * 4 + xh * 2 + 1 - core
-    twin = z * 4 + (1 - xh) * 2 + core
-    core_copies = [
-        remote(part_b.at[block(i * 2 + 1 - core)], core_got.at[i], sibling, tp) for i in range(2)
-    ]
+    for g in range(2):
+        cols = pl.ds(g * half, half)
+        chip_copies[g].wait_recv()
+        whole = part[block(b), cols] + core_got[g, xh].astype(F32) + chip_got[g].astype(F32)
+        grad_hidden[:, cols] = whole
+        whole = whole * short[0, :, cols]
+        grad_mix[:, cols] = whole
+        half_to_channels(whole, GRAD_MIX, g)
+        spread(GRAD_MIX, g)
+    tails[24, :] = jnp.sum(grad_mix[...] * gated[...], axis=0)
 
     arrive(MIXING)
     mixing[...] = to_tokens(MIXING) + skip[...] * gated[...]
     hid[block(b), :] = (short[0] * mixing[...]).astype(BF16)
-
-    landed(core_copies)
-    chip_sent[...] = (part[block((1 - xh) * 2 + core), :] + core_got[1 - xh].astype(F32)).astype(BF16)
-    chip_copy = remote(chip_sent, chip_got, twin, tp)
+    hid_sib = remote(hid.at[block(b)], hid.at[block(b)], sibling, tp)
     hid_twin = remote(hid.at[block(b)], hid.at[block(b)], twin, tp)
-    hid_sib = remote(hid.at[block(b)], hid.at[block(b)], sibling, tp)
-
-    chip_copy.wait_recv()
-    grad_hidden[...] = (
-        part[block(b), :] + core_got[xh].astype(F32) + chip_got[...].astype(F32)
-    )
-    grad_mix[...] = grad_hidden[...] * short[0]
-    to_channels(grad_mix[...], GRAD_MIX)
-    spread(GRAD_MIX)
-
-    hid_twin.wait_recv()
-    other_b = (1 - xh) * 2 + core
-    hid_far = remote(hid.at[block(other_b)], hid.at[block(other_b)], sibling, tp)
     gext[0, :seq] = grad_hidden[...] * mixing[...]
     halo_q = remote(gext.at[0, pl.ds(0, 8)], gext.at[0, pl.ds(seq, 8)], preceding, tp)
+
+    def project(h):
+        pair = block(h, 2 * seq)
+        copies = []
+        for r in list(range(1, ny)) + [0]:
+            oy = lax.rem(y + r, ny)
+            piece = mm(hid[pair, :], wide[:, lanes(oy, 256)])
+            if r == 0:
+                part[pair, lanes(oy, 256)] = piece
+            else:
+                rows_b[pair, lanes(oy, 256)] = piece.astype(BF16)
+                copies.append(
+                    remote(rows_b.at[pair, lanes(oy, 256)], rows_got.at[r - 1, pair], me, oy * 2 + xl)
+                )
+        return copies
+
+    hid_sib.wait_recv()
+    rows_near = project(xh)
+
+    for g in range(2):
+        arrive(GRAD_MIX, g)
+    forward(GRAD_MIX, spec_d)
+    inverse(spec_h, spec_d, True, GRAD_GATED)
+    spread(GRAD_GATED)
+
+    hid_twin.wait_recv()
+    hid_far = remote(hid.at[block(far)], hid.at[block(far)], sibling, tp)
 
     def tap_sums(i):
         grads = gext[i, :seq]
@@ -315,56 +376,47 @@
             tails[8 * i + o, :] = jnp.sum(grads * ext[i, pl.ds(8 - o, seq)], axis=0)
 
     tap_sums(0)
-    tails[24, :] = jnp.sum(grad_mix[...] * gated[...], axis=0)
-
-    hid_sib.wait_recv()
     hid_far.wait_recv()
-
-    def out_columns(i, carry):
-        part[:, lanes(i, 256)] = mm(hid[...], wide[:, lanes(i, 256)])
-        rows_b[:, lanes(i, 256)] = part[:, lanes(i, 256)].astype(BF16)
-        return carry
-
-    lax.fori_loop(0, wide.shape[1] // 256, out_columns, 0)
-    rows_copies = [
-        remote(rows_b.at[:, lanes(oy, 256)], rows_got.at[r], me, oy * 2 + ox)
-        for r, (oy, ox) in enumerate(others[1:])
-    ]
-
-    arrive(GRAD_MIX)
-    forward(GRAD_MIX, spec_d)
-    inverse(spec_h, spec_d, True, GRAD_GATED)
-    spread(GRAD_GATED)
-
-    landed(rows_copies)
-    total = part[:, lanes(y, 256)]
-    for r in range(len(rows_copies)):
-        total += rows_got[r].astype(F32)
-    part[:, lanes(y, 256)] = total
-    pair_sent[...] = part[:, lanes(y * 2 + 1 - xl)]
-    pair_copy = remote(pair_sent, pair_got, me, y * 2 + 1 - xl)
-
+    rows_far = project(1 - xh)
     inverse(spec_u, spec_d, True, GRAD_FILTER)
     spread(GRAD_FILTER)
 
-    pair_copy.wait_recv()
-    final_b[...] = (part[:, lanes(tp)] + pair_got[...]).astype(BF16)
-    mixed_out[:, lanes(b)] = final_b[block(b), :]
-    final_copies = []
-    for r in range(1, 4):
-        other, ctx = mate(r)
-        final_copies.append(remote(final_b.at[block(other)], mixed_out.at[:, lanes(b)], ctx, tp))
-
-    def returned(i, out):
+    def collect(h, copies):
+        pair = block(h, 2 * seq)
+        landed(copies)
+        for r in range(ny - 1):
+            part[pair, lanes(y, 256)] += rows_got[r, pair].astype(F32)
+        pair_sent[pair] = part[pair, lanes(y * 2 + 1 - xl)].astype(BF16)
+        return remote(pair_sent.at[pair], pair_got.at[pair], me, y * 2 + 1 - xl)
+
+    def finish(h, copy):
+        pair = block(h, 2 * seq)
+        copy.wait_recv()
+        final_b[pair] = (part[pair, lanes(tp)] + pair_got[pair].astype(F32)).astype(BF16)
+
+    def hand(other):
+        return remote(final_b.at[block(other)], mixed_out.at[:, lanes(b)], z * 4 + other, tp)
+
+    pair_near = collect(xh, rows_near)
+
+    out_copies = []
+
+    def store(src, dst):
+        copy = pltpu.make_async_copy(src, dst, out_sem.at[len(out_copies)])
+        copy.start()
+        out_copies.append(copy)
+
+    def returned(i, hbm):
         gext[i, seq:] = jnp.where(me == n - 1, 0.0, gext[i, seq:])
-        out[...] = (
+        out_grads[i] = (
             taps[i][0:1] * gext[i, pl.ds(0, seq)]
             + taps[i][1:2] * gext[i, pl.ds(1, seq)]
             + taps[i][2:3] * gext[i, pl.ds(2, seq)]
         ).astype(BF16)
+        store(out_grads.at[i], hbm)
 
     halo_q.wait_recv()
-    returned(0, out_q)
+    returned(0, grad_q_hbm)
 
     arrive(GRAD_GATED)
     grad = to_tokens(GRAD_GATED) + skip[...] * grad_mix[...]
@@ -406,27 +458,59 @@
     mine = (block(lax.div(me, across), 8), lanes(lax.rem(me, across)))
     lax.fori_loop(1, n, hand_in, 0)
     tails_got[block(me, 8), :] = tails[mine]
+
+    pair_far = collect(1 - xh, rows_far)
+    finish(xh, pair_near)
+    mixed_out[:, lanes(b)] = final_b[block(b), :]
+    final_copies = [hand(xh * 2 + 1 - core)]
+
     tails_wait(a2a_recv.at[6])
     tails_sum[mine] = jnp.sum(tails_got[...].reshape(n, 8, 128), axis=0)
     lax.fori_loop(1, n, hand_out, 0)
 
     landed(halo_kv)
-    returned(1, out_k)
-    returned(2, out_v)
+    returned(1, grad_k_hbm)
+    returned(2, grad_v_hbm)
+    finish(1 - xh, pair_far)
+    final_copies += [hand(far), hand((1 - xh) * 2 + 1 - core)]
     arrive(GRAD_FILTER)
     out_filter[...] = to_tokens(GRAD_FILTER).astype(BF16)
+    store(out_filter, filter_hbm)
 
     tails_wait(a2a_recv.at[7])
     for i in range(3):
         out_short[i] = tails_sum[8 * i : 8 * i + 3, :]
     out_skip[...] = tails_sum[24:25, :]
+    store(out_short, short_hbm)
+    store(out_skip, skip_hbm)
     landed(final_copies)
+    store(mixed_out, mixed_hbm)
     for copy in pending:
         copy.wait_send()
-    for k in range(6):
+    for k in (FILTER, GATED, MIXING, GRAD_GATED, GRAD_FILTER):
         left(k)
+    for g in range(2):
+        left(GRAD_MIX, g)
     tails_wait(a2a_send.at[6])
     tails_wait(a2a_send.at[7])
+    for copy in out_copies:
+        copy.wait()
+
+
+def handover(*refs):
+    count = 7
+    sources, targets, held = refs[:count], refs[count : 2 * count], refs[2 * count : 3 * count]
+    in_sem, out_sem = refs[3 * count :]
+    copies = [pltpu.make_async_copy(sources[i], held[i], in_sem.at[i]) for i in range(count)]
+    for copy in copies:
+        copy.start()
+    outs = []
+    for i in range(count):
+        copies[i].wait()
+        outs.append(pltpu.make_async_copy(held[i], targets[i], out_sem.at[i]))
+        outs[-1].start()
+    for copy in outs:
+        copy.wait()
 
 
 def local(*args):
@@ -439,11 +523,15 @@
     q_rows = GROUP * (n + 1)
     d_cols = nz * 128
     tokens4 = 4 * seq
+    half = ch // 2
 
     def vmem(shape, dtype=F32):
         return pltpu.VMEM(shape, dtype)
 
     scratch = [
+        vmem((seq, ch), BF16), vmem((seq, ch), BF16), vmem((seq, ch), BF16), vmem((seq, ch)),
+        vmem(cot.shape, BF16), vmem((3, seq, ch), BF16), vmem((seq, ch), BF16),
+        vmem((1, ch)), vmem((3, 3, ch)),
         vmem(outer.shape, BF16), vmem(outer_back.shape, BF16), vmem(inner.shape, BF16),
         vmem(twiddle.shape),
         vmem((3, 16, ch), BF16), vmem((3, seq + 8, ch)), vmem((3, seq, ch)),
@@ -452,16 +540,16 @@
         vmem((6, 16 * n, 2 * seq), BF16), vmem((6, 16 * n, 2 * seq), BF16),
         vmem((ch, d_cols), BF16), vmem((tokens4, d_cols), BF16),
         vmem((tokens4, max(ch, d_cols))), vmem((tokens4, ch), BF16),
-        vmem((2, seq, ch), BF16), vmem((seq, ch), BF16), vmem((seq, ch), BF16),
+        vmem((2, 2, seq, half), BF16), vmem((2, seq, half), BF16), vmem((2, seq, half), BF16),
         vmem((tokens4, ch), BF16),
         vmem((tokens4, d_cols), BF16), vmem((max(ny - 1, 1), tokens4, 256), BF16),
-        vmem((tokens4, 128)), vmem((tokens4, 128)), vmem((tokens4, 128), BF16),
+        vmem((tokens4, 128), BF16), vmem((tokens4, 128), BF16), vmem((tokens4, 128), BF16),
         vmem((2, q_rows, 2 * seq)), vmem((2, q_rows, 2 * seq)), vmem((2, q_rows, 2 * seq)),
         vmem((2 * n * GROUP, 2 * seq)),
         vmem((32, ch)), vmem((8 * n, 128)), vmem((32, ch)),
-        pltpu.SemaphoreType.DMA((4,)),
-        pltpu.SemaphoreType.DMA((8,)), pltpu.SemaphoreType.DMA((8,)),
-        pltpu.SemaphoreType.DMA((48,)), pltpu.SemaphoreType.DMA((48,)),
+        pltpu.SemaphoreType.DMA((4,)), pltpu.SemaphoreType.DMA((6,)), pltpu.SemaphoreType.DMA((7,)),
+        pltpu.SemaphoreType.DMA((10,)), pltpu.SemaphoreType.DMA((10,)),
+        pltpu.SemaphoreType.DMA((64,)), pltpu.SemaphoreType.DMA((64,)),
     ]
     shape = jax.ShapeDtypeStruct
     inside = pl.BlockSpec(memory_space=pltpu.VMEM)
@@ -475,14 +563,23 @@
     results = pl.pallas_call(
         lambda *refs: body(n, nz, ny, refs),
         out_shape=out_shape,
-        in_specs=[inside] * 10 + [outside] * 4,
-        out_specs=[inside] * 7,
+        in_specs=[outside] * 3 + [inside] * 3 + [outside, inside, outside, outside] + [outside] * 4,
+        out_specs=[outside] * 7,
         scratch_shapes=scratch,
         compiler_params=pltpu.CompilerParams(
             collective_id=0, has_side_effects=True, vmem_limit_bytes=60 * 1024 * 1024
         ),
         name="hyena",
     )(query, key, value, tap_q, tap_k, tap_v, filt, skip.reshape(1, ch), weight, cot, *consts)
+    results = pl.pallas_call(
+        handover,
+        out_shape=out_shape,
+        in_specs=[outside] * 7,
+        out_specs=[outside] * 7,
+        scratch_shapes=[vmem(o.shape, o.dtype) for o in out_shape]
+        + [pltpu.SemaphoreType.DMA((7,)), pltpu.SemaphoreType.DMA((7,))],
+        name="handover",
+    )(*results)
     return results[:5] + (results[5].reshape(ch), results[6])
 
 

time: 128 us -> 104 us (0.81)
  Pallas kernels: 118 us -> 103 us
  local copies, waits for them, and re-layouts: 9.48 us -> 0 us
    pallas_call x1, Pallas kernels: 118 us -> 101 us  [local(): pl.pallas_call(lambda *refs: body(n, nz, ny, refs), out_shape=out_shape,...]
    unnamed x11 -> x0, local copies, waits for them, and re-layouts: 9.48 us -> none
    pallas_call x0 -> x1, Pallas kernels: none -> 2.11 us  [local(): pl.pallas_call(handover, out_shape=out_shape, in_specs=[outside] * 7, out...]
where the time goes in v2:
time: 104 us
  Pallas kernels  103 us (99%)
    pallas_call x1, Pallas kernels, local(): pl.pallas_call(lambda *refs: body(n, nz, ny, refs), out_shape=out_shape,...  101 us
    pallas_call x1, Pallas kernels, local(): pl.pallas_call(handover, out_shape=out_shape, in_specs=[outside] * 7, out...  2.11 us

profile of v2, /device:TPU:1, one launch (start us, length us, event | category | flops | bytes accessed | tf_op | source)
XLA Modules:
  0.0 103.8 jit_solution(16363148799796645517)
XLA Ops:
  0.6 100.9 %hyena.1 = (bf16[128,512]{1,0:T(8,128)(2,1)}, bf16[128,1024]{1,0:T(8,128)(2,1)}, bf16[128,1024]{1,0:T(8,128)(2,1)}, bf16[128,1024]{1,0:T(8,128)(2,1)}, bf16[128,...) custom-call(bf16[128,1024]{1,0:T(8,128)(2,1)} %refs_0_.1, bf16[128,1024]{1,0:T(8,128)(2,1)} %refs_1_.1, ...), custom_call_target="tpu_custom_call" | custom-call | tf_op jit(solution)/shard_map/hyena/pallas_call | solution.py:563
  101.5 2.1 %handover.1 = (bf16[128,512]{1,0:T(8,128)(2,1)}, bf16[128,1024]{1,0:T(8,128)(2,1)}, bf16[128,1024]{1,0:T(8,128)(2,1)}, bf16[128,1024]{1,0:T(8,128)(2,1)}, bf16[1...) custom-call(bf16[128,512]{1,0:T(8,128)(2,1)} %get-tuple-element.21.refs_0_, ...), custom_call_target="tpu_custom_call" | custom-call | tf_op jit(solution)/shard_map/handover/pallas_call | solution.py:574

commit v3 on v2

--- a/solution.py
+++ b/solution.py
@@ -11,6 +11,7 @@
 BF16 = jnp.bfloat16
 GROUP = 16
 FILTER, GATED, MIXING, GRAD_MIX, GRAD_GATED, GRAD_FILTER = range(6)
+FILTER_PLACE, GATED_PLACE, ORDER, LATE_FILTER = 0, 4, 2, False
 
 
 def halves(matrix):
@@ -100,12 +101,16 @@
         size = seq if size is None else size
         return pl.ds(pl.multiple_of(index * size, size), size)
 
+    def peer(r):
+        off = lax.div(r, 2)
+        return lax.rem(me + n // 2 + off * (1 - 2 * lax.rem(r, 2)) + n, n)
+
     def spread(k, g=None):
         cols = pl.ds(0, 2 * seq) if g is None else pl.ds(g * seq, seq)
         sem = k if g is None else 8 + g
 
         def step(r, carry):
-            dst = lax.rem(me + r, n)
+            dst = peer(r)
             pltpu.make_async_remote_copy(
                 src_ref=sent.at[k, at16(dst), cols], dst_ref=got.at[k, at16(me), cols],
                 send_sem=a2a_send.at[sem], recv_sem=a2a_recv.at[sem],
@@ -247,11 +252,17 @@
             landed(hops[c])
             hops[c] = ring(s, c) if s <= full else []
 
+    def send_at(place):
+        if place == FILTER_PLACE:
+            spread(FILTER)
+        if place == GATED_PLACE:
+            spread(GATED)
+
     cot_first = []
     for r in range(1, 4):
         other, ctx = mate(r)
         cot_first.append(remote(cot.at[:, lanes(other)], cots.at[block(b), lanes(tp)], ctx, tp))
-    spread(FILTER)
+    send_at(0)
 
     for copy in loads[1:]:
         copy.wait()
@@ -270,8 +281,10 @@
 
     landed(cot_first)
     cot_pair = remote(cots.at[:, lanes(tp)], cots.at[:, lanes(tp)], me, y * 2 + 1 - xl)
+    send_at(1)
     for s in range(1, full):
         advance(s)
+        send_at(1 + s)
         if s == 1:
             cot_pair.wait_recv()
             cot_last = [
@@ -285,33 +298,52 @@
             for oy, ox in others[1:]
         ]
 
+    def slots(offsets):
+        places = [lax.rem(z + nz + o, nz) for o in offsets]
+        return (
+            jnp.concatenate([cots[:, lanes(p)] for p in places], axis=1),
+            lambda some: jnp.concatenate([wide[some, lanes(p)] for p in places], axis=1),
+        )
+
+    def add_slots(offsets, first):
+        tokens, features = slots(offsets)
+        for lo in range(0, ch, 256):
+            some = pl.ds(lo, 256)
+            term = lax.dot_general(
+                tokens, features(some), (((1,), (1,)), ((), ())), preferred_element_type=F32
+            )
+            part[:, some] = term if first else part[:, some] + term
+
+    if full > 0:
+        advance(full)
+    send_at(4)
+    landed(cot_last)
+    add_slots([0] + [o * w for o in range(1, full + 1) for w in (1, -1)], True)
     for copy in consts:
         copy.wait()
-    arrive(FILTER)
-    forward(FILTER, spec_h)
-    if full > 0:
-        advance(full)
-    spread(GATED)
+    if FILTER_PLACE < 2:
+        arrive(FILTER)
+        forward(FILTER, spec_h)
 
     advance(full + 1)
-    landed(cot_last)
     sibling = z * 4 + xh * 2 + 1 - core
     twin = z * 4 + (1 - xh) * 2 + core
     far = (1 - xh) * 2 + core
     core_copies = []
+    tokens, features = slots([full + 1])
     for g in range(2):
         cols = pl.ds(g * half, half)
-        for lo in range(g * half, (g + 1) * half, 256) if half >= 256 else [g * half]:
-            some = pl.ds(lo, min(256, half))
-            part[:, some] = lax.dot_general(
-                cots[...], wide[some, :], (((1,), (1,)), ((), ())), preferred_element_type=F32
-            )
+        term = lax.dot_general(
+            tokens, features(cols), (((1,), (1,)), ((), ())), preferred_element_type=F32
+        )
+        part[:, cols] += term
         for i in range(2):
             theirs = block(i * 2 + 1 - core)
             part_b[theirs, cols] = part[theirs, cols].astype(BF16)
         core_copies.append(
             [remote(part_b.at[block(i * 2 + 1 - core), cols], core_got.at[g, i], sibling, tp) for i in range(2)]
         )
+    send_at(5)
     chip_copies = []
     for g in range(2):
         cols = pl.ds(g * half, half)
@@ -319,10 +351,18 @@
         chip_sent[g] = (part[block(far), cols] + core_got[g, 1 - xh].astype(F32)).astype(BF16)
         chip_copies.append(remote(chip_sent.at[g], chip_got.at[g], twin, tp))
 
-    arrive(GATED)
-    forward(GATED, spec_u)
-    inverse(spec_h, spec_u, False, MIXING)
-    spread(MIXING)
+    def mix(first, second):
+        if first:
+            arrive(GATED)
+            forward(GATED, spec_u)
+        if second:
+            inverse(spec_h, spec_u, False, MIXING)
+            spread(MIXING)
+
+    if FILTER_PLACE >= 2 and ORDER != 0:
+        arrive(FILTER)
+        forward(FILTER, spec_h)
+    mix(ORDER != 0, ORDER == 2)
 
     for g in range(2):
         cols = pl.ds(g * half, half)
@@ -333,13 +373,30 @@
         grad_mix[:, cols] = whole
         half_to_channels(whole, GRAD_MIX, g)
         spread(GRAD_MIX, g)
-    tails[24, :] = jnp.sum(grad_mix[...] * gated[...], axis=0)
+    if FILTER_PLACE >= 2 and ORDER == 0:
+        arrive(FILTER)
+        forward(FILTER, spec_h)
+    mix(ORDER == 0, ORDER != 2)
+    tails[3, :] = jnp.sum(grad_mix[...] * gated[...], axis=0)
+
+    def back():
+        for g in range(2):
+            arrive(GRAD_MIX, g)
+        forward(GRAD_MIX, spec_d)
+        inverse(spec_h, spec_d, True, GRAD_GATED)
+        spread(GRAD_GATED)
+
+    if ORDER != 2:
+        back()
 
     arrive(MIXING)
     mixing[...] = to_tokens(MIXING) + skip[...] * gated[...]
     hid[block(b), :] = (short[0] * mixing[...]).astype(BF16)
     hid_sib = remote(hid.at[block(b)], hid.at[block(b)], sibling, tp)
-    hid_twin = remote(hid.at[block(b)], hid.at[block(b)], twin, tp)
+    hid_twin = [
+        remote(hid.at[block(b), pl.ds(g * half, half)], hid.at[block(b), pl.ds(g * half, half)], twin, tp)
+        for g in range(2)
+    ]
     gext[0, :seq] = grad_hidden[...] * mixing[...]
     halo_q = remote(gext.at[0, pl.ds(0, 8)], gext.at[0, pl.ds(seq, 8)], preceding, tp)
 
@@ -361,25 +418,79 @@
     hid_sib.wait_recv()
     rows_near = project(xh)
 
+    if ORDER == 2:
+        back()
+
+    hid_far = []
     for g in range(2):
-        arrive(GRAD_MIX, g)
-    forward(GRAD_MIX, spec_d)
-    inverse(spec_h, spec_d, True, GRAD_GATED)
-    spread(GRAD_GATED)
-
-    hid_twin.wait_recv()
-    hid_far = remote(hid.at[block(far)], hid.at[block(far)], sibling, tp)
+        hid_twin[g].wait_recv()
+        place = hid.at[block(far), pl.ds(g * half, half)]
+        hid_far.append(remote(place, place, sibling, tp))
+
+    def hand_in(g):
+        def step(r, carry):
+            to_z = lax.rem(z + r, nz)
+            dst = to_z * 4 + 3 - 3 * g
+
+            @pl.when(dst != me)
+            def _():
+                pltpu.make_async_remote_copy(
+                    src_ref=tails.at[pl.ds(8 * g, 8), lanes(to_z)], dst_ref=tails_got.at[g, block(me, 8)],
+                    send_sem=a2a_send.at[6 + g], recv_sem=a2a_recv.at[6 + g],
+                    device_id=(dst, tp), device_id_type=pl.DeviceIdType.MESH,
+                ).start()
+
+            return carry
+
+        lax.fori_loop(0, nz, step, 0)
+        tails_got[g, block(me, 8), :] = tails[8 * g : 8 * g + 8, lanes(z)]
+
+    def tails_wait(sem, count):
+        whole = tails_got.at[0, pl.ds(0, 8 * count)]
+        pltpu.make_async_copy(whole, whole, sem).wait()
+
+    def owner_wait(g, sem, count, other):
+        owner = b == 3 - 3 * g
+
+        @pl.when(owner)
+        def _():
+            tails_wait(sem, count)
+
+        if other:
+            @pl.when(jnp.logical_not(owner))
+            def _():
+                tails_wait(sem, other)
+
+    def hand_out(g):
+        place = tails_sum.at[pl.ds(8 * g, 8), lanes(z)]
+
+        @pl.when(b == 3 - 3 * g)
+        def _():
+            tails_wait(a2a_recv.at[6 + g], n - 1)
+            tails_sum[8 * g : 8 * g + 8, lanes(z)] = jnp.sum(tails_got[g].reshape(n, 8, 128), axis=0)
+
+            def step(r, carry):
+                pltpu.make_async_remote_copy(
+                    src_ref=place, dst_ref=place,
+                    send_sem=a2a_send.at[10 + g], recv_sem=a2a_recv.at[10 + g],
+                    device_id=(peer(r), tp), device_id_type=pl.DeviceIdType.MESH,
+                ).start()
+                return carry
+
+            lax.fori_loop(1, n, step, 0)
 
     def tap_sums(i):
         grads = gext[i, :seq]
         for o in range(3):
-            tails[8 * i + o, :] = jnp.sum(grads * ext[i, pl.ds(8 - o, seq)], axis=0)
+            tails[(0, 8, 11)[i] + o, :] = jnp.sum(grads * ext[i, pl.ds(8 - o, seq)], axis=0)
 
     tap_sums(0)
-    hid_far.wait_recv()
+    hand_in(0)
+    landed(hid_far)
     rows_far = project(1 - xh)
     inverse(spec_u, spec_d, True, GRAD_FILTER)
-    spread(GRAD_FILTER)
+    if not LATE_FILTER:
+        spread(GRAD_FILTER)
 
     def collect(h, copies):
         pair = block(h, 2 * seq)
@@ -417,8 +528,11 @@
 
     halo_q.wait_recv()
     returned(0, grad_q_hbm)
+    hand_out(0)
 
     arrive(GRAD_GATED)
+    if LATE_FILTER:
+        spread(GRAD_FILTER)
     grad = to_tokens(GRAD_GATED) + skip[...] * grad_mix[...]
     gext[1, :seq] = grad * short[2]
     gext[2, :seq] = grad * short[1]
@@ -428,45 +542,14 @@
     tap_sums(1)
     tap_sums(2)
 
-    across = ch // 128
-
-    def tile(ref, d):
-        return ref.at[block(lax.div(d, across), 8), lanes(lax.rem(d, across))]
-
-    def hand_in(r, carry):
-        dst = lax.rem(me + r, n)
-        pltpu.make_async_remote_copy(
-            src_ref=tile(tails, dst), dst_ref=tails_got.at[block(me, 8)],
-            send_sem=a2a_send.at[6], recv_sem=a2a_recv.at[6],
-            device_id=(dst, tp), device_id_type=pl.DeviceIdType.MESH,
-        ).start()
-        return carry
-
-    def hand_out(r, carry):
-        dst = lax.rem(me + r, n)
-        pltpu.make_async_remote_copy(
-            src_ref=tile(tails_sum, me), dst_ref=tile(tails_sum, me),
-            send_sem=a2a_send.at[7], recv_sem=a2a_recv.at[7],
-            device_id=(dst, tp), device_id_type=pl.DeviceIdType.MESH,
-        ).start()
-        return carry
-
-    def tails_wait(sem):
-        whole = tails_got.at[pl.ds(0, 8 * (n - 1))]
-        pltpu.make_async_copy(whole, whole, sem).wait()
-
-    mine = (block(lax.div(me, across), 8), lanes(lax.rem(me, across)))
-    lax.fori_loop(1, n, hand_in, 0)
-    tails_got[block(me, 8), :] = tails[mine]
+    hand_in(1)
 
     pair_far = collect(1 - xh, rows_far)
     finish(xh, pair_near)
     mixed_out[:, lanes(b)] = final_b[block(b), :]
     final_copies = [hand(xh * 2 + 1 - core)]
 
-    tails_wait(a2a_recv.at[6])
-    tails_sum[mine] = jnp.sum(tails_got[...].reshape(n, 8, 128), axis=0)
-    lax.fori_loop(1, n, hand_out, 0)
+    hand_out(1)
 
     landed(halo_kv)
     returned(1, grad_k_hbm)
@@ -477,10 +560,11 @@
     out_filter[...] = to_tokens(GRAD_FILTER).astype(BF16)
     store(out_filter, filter_hbm)
 
-    tails_wait(a2a_recv.at[7])
-    for i in range(3):
-        out_short[i] = tails_sum[8 * i : 8 * i + 3, :]
-    out_skip[...] = tails_sum[24:25, :]
+    for g in range(2):
+        owner_wait(g, a2a_recv.at[10 + g], nz - 1, nz)
+    for i, row in enumerate((0, 8, 11)):
+        out_short[i] = tails_sum[row : row + 3, :]
+    out_skip[...] = tails_sum[3:4, :]
     store(out_short, short_hbm)
     store(out_skip, skip_hbm)
     landed(final_copies)
@@ -491,8 +575,9 @@
         left(k)
     for g in range(2):
         left(GRAD_MIX, g)
-    tails_wait(a2a_send.at[6])
-    tails_wait(a2a_send.at[7])
+    for g in range(2):
+        owner_wait(g, a2a_send.at[6 + g], nz - 1, nz)
+        owner_wait(g, a2a_send.at[10 + g], n - 1, 0)
     for copy in out_copies:
         copy.wait()
 
@@ -546,9 +631,9 @@
         vmem((tokens4, 128), BF16), vmem((tokens4, 128), BF16), vmem((tokens4, 128), BF16),
         vmem((2, q_rows, 2 * seq)), vmem((2, q_rows, 2 * seq)), vmem((2, q_rows, 2 * seq)),
         vmem((2 * n * GROUP, 2 * seq)),
-        vmem((32, ch)), vmem((8 * n, 128)), vmem((32, ch)),
+        vmem((16, ch)), vmem((2, 8 * n, 128)), vmem((16, ch)),
         pltpu.SemaphoreType.DMA((4,)), pltpu.SemaphoreType.DMA((6,)), pltpu.SemaphoreType.DMA((7,)),
-        pltpu.SemaphoreType.DMA((10,)), pltpu.SemaphoreType.DMA((10,)),
+        pltpu.SemaphoreType.DMA((12,)), pltpu.SemaphoreType.DMA((12,)),
         pltpu.SemaphoreType.DMA((64,)), pltpu.SemaphoreType.DMA((64,)),
     ]
     shape = jax.ShapeDtypeStruct

time: 104 us -> 101 us (0.971)
  Pallas kernels: 103 us -> 100 us
    pallas_call x1, Pallas kernels: 101 us -> 98 us  [local(): pl.pallas_call(lambda *refs: body(n, nz, ny, refs), out_shape=out_shape,...]
where the time goes in v3:
time: 101 us
  Pallas kernels  100 us (99%)
    pallas_call x1, Pallas kernels, local(): pl.pallas_call(lambda *refs: body(n, nz, ny, refs), out_shape=out_shape,...  98 us
    pallas_call x1, Pallas kernels, local(): pl.pallas_call(handover, out_shape=out_shape, in_specs=[outside] * 7, out...  2.11 us

profile of v3, /device:TPU:1, one launch (start us, length us, event | category | flops | bytes accessed | tf_op | source)
XLA Modules:
  0.0 100.9 jit_solution(467016618929332391)
XLA Ops:
  0.6 98.0 %hyena.1 = (bf16[128,512]{1,0:T(8,128)(2,1)}, bf16[128,1024]{1,0:T(8,128)(2,1)}, bf16[128,1024]{1,0:T(8,128)(2,1)}, bf16[128,1024]{1,0:T(8,128)(2,1)}, bf16[128,...) custom-call(bf16[128,1024]{1,0:T(8,128)(2,1)} %refs_0_.1, bf16[128,1024]{1,0:T(8,128)(2,1)} %refs_1_.1, ...), custom_call_target="tpu_custom_call" | custom-call | tf_op jit(solution)/shard_map/hyena/pallas_call | solution.py:648
  98.6 2.1 %handover.1 = (bf16[128,512]{1,0:T(8,128)(2,1)}, bf16[128,1024]{1,0:T(8,128)(2,1)}, bf16[128,1024]{1,0:T(8,128)(2,1)}, bf16[128,1024]{1,0:T(8,128)(2,1)}, bf16[1...) custom-call(bf16[128,512]{1,0:T(8,128)(2,1)} %get-tuple-element.21.refs_0_, ...), custom_call_target="tpu_custom_call" | custom-call | tf_op jit(solution)/shard_map/handover/pallas_call | solution.py:659

commit v4 on v3

--- a/solution.py
+++ b/solution.py
@@ -11,7 +11,8 @@
 BF16 = jnp.bfloat16
 GROUP = 16
 FILTER, GATED, MIXING, GRAD_MIX, GRAD_GATED, GRAD_FILTER = range(6)
-FILTER_PLACE, GATED_PLACE, ORDER, LATE_FILTER = 0, 4, 2, False
+FILTER_PLACE, GATED_PLACE, ORDER, LATE_FILTER = 0, 3, 2, False
+EARLY_FAR, SINGLE = False, True
 
 
 def halves(matrix):
@@ -211,16 +212,7 @@
     ]
     for copy in consts:
         copy.start()
-    tails[...] = jnp.zeros_like(tails)
-    loads[0].wait()
-    to_channels(filt[...], FILTER)
     pl.semaphore_wait(barrier, n - 1 + len(others))
-
-    following, preceding = lax.rem(me + 1, n), lax.rem(me + n - 1, n)
-    halos = [
-        remote(x.at[pl.ds(seq - 16, 16)], halo.at[i], following, tp)
-        for i, x in enumerate((query_hbm, key_hbm, value_hbm))
-    ]
 
     full = nz // 2 - 1
     up, down = lax.rem(z + 1, nz) * 4 + b, lax.rem(z + nz - 1, nz) * 4 + b
@@ -247,6 +239,12 @@
 
     hops = [ring(0, c) for c in range(2)]
 
+    following, preceding = lax.rem(me + 1, n), lax.rem(me + n - 1, n)
+    halos = [
+        remote(x.at[pl.ds(seq - 16, 16)], halo.at[i], following, tp)
+        for i, x in enumerate((query_hbm, key_hbm, value_hbm))
+    ]
+
     def advance(s):
         for c in range(2):
             landed(hops[c])
@@ -262,8 +260,11 @@
     for r in range(1, 4):
         other, ctx = mate(r)
         cot_first.append(remote(cot.at[:, lanes(other)], cots.at[block(b), lanes(tp)], ctx, tp))
+    loads[0].wait()
+    to_channels(filt[...], FILTER)
     send_at(0)
 
+    tails[...] = jnp.zeros_like(tails)
     for copy in loads[1:]:
         copy.wait()
     landed(halos)
@@ -372,17 +373,30 @@
         whole = whole * short[0, :, cols]
         grad_mix[:, cols] = whole
         half_to_channels(whole, GRAD_MIX, g)
-        spread(GRAD_MIX, g)
+        if not SINGLE:
+            spread(GRAD_MIX, g)
+    if SINGLE:
+        spread(GRAD_MIX)
     if FILTER_PLACE >= 2 and ORDER == 0:
         arrive(FILTER)
         forward(FILTER, spec_h)
     mix(ORDER == 0, ORDER != 2)
     tails[3, :] = jnp.sum(grad_mix[...] * gated[...], axis=0)
 
+    hid_far = []
+
+    def relay():
+        for g in range(2):
+            hid_twin[g].wait_recv()
+            place = hid.at[block(far), pl.ds(g * half, half)]
+            hid_far.append(remote(place, place, sibling, tp))
+
     def back():
-        for g in range(2):
+        for g in (None,) if SINGLE else range(2):
             arrive(GRAD_MIX, g)
         forward(GRAD_MIX, spec_d)
+        if EARLY_FAR:
+            relay()
         inverse(spec_h, spec_d, True, GRAD_GATED)
         spread(GRAD_GATED)
 
@@ -421,11 +435,11 @@
     if ORDER == 2:
         back()
 
-    hid_far = []
-    for g in range(2):
-        hid_twin[g].wait_recv()
-        place = hid.at[block(far), pl.ds(g * half, half)]
-        hid_far.append(remote(place, place, sibling, tp))
+    if not EARLY_FAR:
+        relay()
+    else:
+        landed(hid_far)
+        rows_far = project(1 - xh)
 
     def hand_in(g):
         def step(r, carry):
@@ -486,8 +500,9 @@
 
     tap_sums(0)
     hand_in(0)
-    landed(hid_far)
-    rows_far = project(1 - xh)
+    if not EARLY_FAR:
+        landed(hid_far)
+        rows_far = project(1 - xh)
     inverse(spec_u, spec_d, True, GRAD_FILTER)
     if not LATE_FILTER:
         spread(GRAD_FILTER)
@@ -573,7 +588,7 @@
         copy.wait_send()
     for k in (FILTER, GATED, MIXING, GRAD_GATED, GRAD_FILTER):
         left(k)
-    for g in range(2):
+    for g in (None,) if SINGLE else range(2):
         left(GRAD_MIX, g)
     for g in range(2):
         owner_wait(g, a2a_send.at[6 + g], nz - 1, nz)

time: 101 us -> 98.9 us (0.979)
  Pallas kernels: 100 us -> 97.9 us
    pallas_call x1, Pallas kernels: 98 us -> 95.8 us  [local(): pl.pallas_call(lambda *refs: body(n, nz, ny, refs), out_shape=out_shape,...]
where the time goes in v4:
time: 98.9 us; the launch traced here: 98.7 us
  Pallas kernels  97.9 us (99%)
    pallas_call x1, Pallas kernels, local(): pl.pallas_call(lambda *refs: body(n, nz, ny, refs), out_shape=out_shape,...  95.8 us
    pallas_call x1, Pallas kernels, local(): pl.pallas_call(handover, out_shape=out_shape, in_specs=[outside] * 7, out...  2.11 us

profile of v4, /device:TPU:1, one launch (start us, length us, event | category | flops | bytes accessed | tf_op | source)
XLA Modules:
  0.0 98.7 jit_solution(3162665100464331648)
XLA Ops:
  0.6 95.8 %hyena.1 = (bf16[128,512]{1,0:T(8,128)(2,1)}, bf16[128,1024]{1,0:T(8,128)(2,1)}, bf16[128,1024]{1,0:T(8,128)(2,1)}, bf16[128,1024]{1,0:T(8,128)(2,1)}, bf16[128,...) custom-call(bf16[128,1024]{1,0:T(8,128)(2,1)} %refs_0_.1, bf16[128,1024]{1,0:T(8,128)(2,1)} %refs_1_.1, ...), custom_call_target="tpu_custom_call" | custom-call | tf_op jit(solution)/shard_map/hyena/pallas_call | solution.py:663
  96.5 2.1 %handover.1 = (bf16[128,512]{1,0:T(8,128)(2,1)}, bf16[128,1024]{1,0:T(8,128)(2,1)}, bf16[128,1024]{1,0:T(8,128)(2,1)}, bf16[128,1024]{1,0:T(8,128)(2,1)}, bf16[1...) custom-call(bf16[128,512]{1,0:T(8,128)(2,1)} %get-tuple-element.21.refs_0_, ...), custom_call_target="tpu_custom_call" | custom-call | tf_op jit(solution)/shard_map/handover/pallas_call | solution.py:674

commit v5 on v4

--- a/solution.py
+++ b/solution.py
@@ -214,17 +214,18 @@
         copy.start()
     pl.semaphore_wait(barrier, n - 1 + len(others))
 
+    quarter = ch // 4
     full = nz // 2 - 1
     up, down = lax.rem(z + 1, nz) * 4 + b, lax.rem(z + nz - 1, nz) * 4 + b
 
     def ring(s, c):
-        piece = pl.ds(c * half, half)
+        piece = pl.ds(c * quarter, quarter)
         slot_up, slot_down = lanes(lax.rem(z + nz - s, nz)), lanes(lax.rem(z + s, nz))
         copies = []
-        if s < full or c == 0:
+        if s < full or c < 2:
             src = weight.at[piece] if s == 0 else wide.at[piece, slot_up]
             copies.append(remote(src, wide.at[piece, slot_up], up, tp))
-        if s < full or c == 1:
+        if s < full or c >= 2:
             src = weight.at[piece] if s == 0 else wide.at[piece, slot_down]
             copies.append(remote(src, wide.at[piece, slot_down], down, tp))
         return copies
@@ -237,7 +238,7 @@
         other = lax.rem(b + r, 4)
         return other, z * 4 + other
 
-    hops = [ring(0, c) for c in range(2)]
+    hops = [ring(0, c) for c in range(4)]
 
     following, preceding = lax.rem(me + 1, n), lax.rem(me + n - 1, n)
     halos = [
@@ -246,7 +247,7 @@
     ]
 
     def advance(s):
-        for c in range(2):
+        for c in range(4):
             landed(hops[c])
             hops[c] = ring(s, c) if s <= full else []
 
@@ -500,10 +501,10 @@
 
     tap_sums(0)
     hand_in(0)
+    inverse(spec_u, spec_d, True, GRAD_FILTER)
     if not EARLY_FAR:
         landed(hid_far)
         rows_far = project(1 - xh)
-    inverse(spec_u, spec_d, True, GRAD_FILTER)
     if not LATE_FILTER:
         spread(GRAD_FILTER)
 
@@ -649,7 +650,7 @@
         vmem((16, ch)), vmem((2, 8 * n, 128)), vmem((16, ch)),
         pltpu.SemaphoreType.DMA((4,)), pltpu.SemaphoreType.DMA((6,)), pltpu.SemaphoreType.DMA((7,)),
         pltpu.SemaphoreType.DMA((12,)), pltpu.SemaphoreType.DMA((12,)),
-        pltpu.SemaphoreType.DMA((64,)), pltpu.SemaphoreType.DMA((64,)),
+        pltpu.SemaphoreType.DMA((72,)), pltpu.SemaphoreType.DMA((72,)),
     ]
     shape = jax.ShapeDtypeStruct
     inside = pl.BlockSpec(memory_space=pltpu.VMEM)

time: 98.9 us -> 100 us (1.011)
  Pallas kernels: 97.9 us -> 98.9 us
    pallas_call x1, Pallas kernels: 95.8 us -> 96.8 us  [local(): pl.pallas_call(lambda *refs: body(n, nz, ny, refs), out_shape=out_shape,...]
where the time goes in v5:
time: 100 us; the launch traced here: 99.8 us
  Pallas kernels  98.9 us (99%)
    pallas_call x1, Pallas kernels, local(): pl.pallas_call(lambda *refs: body(n, nz, ny, refs), out_shape=out_shape,...  96.8 us
    pallas_call x1, Pallas kernels, local(): pl.pallas_call(handover, out_shape=out_shape, in_specs=[outside] * 7, out...  2.11 us

profile of v5, /device:TPU:1, one launch (start us, length us, event | category | flops | bytes accessed | tf_op | source)
XLA Modules:
  0.0 99.8 jit_solution(9274750531212002902)
XLA Ops:
  0.6 96.8 %hyena.1 = (bf16[128,512]{1,0:T(8,128)(2,1)}, bf16[128,1024]{1,0:T(8,128)(2,1)}, bf16[128,1024]{1,0:T(8,128)(2,1)}, bf16[128,1024]{1,0:T(8,128)(2,1)}, bf16[128,...) custom-call(bf16[128,1024]{1,0:T(8,128)(2,1)} %refs_0_.1, bf16[128,1024]{1,0:T(8,128)(2,1)} %refs_1_.1, ...), custom_call_target="tpu_custom_call" | custom-call | tf_op jit(solution)/shard_map/hyena/pallas_call | solution.py:664
  97.5 2.1 %handover.1 = (bf16[128,512]{1,0:T(8,128)(2,1)}, bf16[128,1024]{1,0:T(8,128)(2,1)}, bf16[128,1024]{1,0:T(8,128)(2,1)}, bf16[128,1024]{1,0:T(8,128)(2,1)}, bf16[1...) custom-call(bf16[128,512]{1,0:T(8,128)(2,1)} %get-tuple-element.21.refs_0_, ...), custom_call_target="tpu_custom_call" | custom-call | tf_op jit(solution)/shard_map/handover/pallas_call | solution.py:675
